TPU v7x, 32 devices: a whole 2x2x4 slice. The times are simulated.
32 devices in a mesh: groups: 2 (over y), wide: 8 (over z, x), narrow: 2 (over core).
Axes of the slice: x: 2, y: 2, z: 4, core: 2. Of those that a mesh axis runs over, the one named last changes fastest.
Arguments:
- act_rows: bfloat16 [96, 7168], P(('groups', 'wide'), 'narrow'), parts along dimension 0, may hold values from -6 to 6
- routes: int32 [96, 3], P(('groups', 'wide')), parts along dimension 0, may hold values from 0 to 47, as said below
- route_weights: float32 [96, 3], P(('groups', 'wide')), parts along dimension 0, may hold values from 0.2 to 1
- owners: int32 [4], replicated, may hold values from 0 to 3, each once
- w_gate: bfloat16 [7168, 20480], P('narrow', 'wide'), may hold values from -0.0625 to 0.0625
- w_up: bfloat16 [7168, 20480], P('narrow', 'wide'), may hold values from -0.0625 to 0.0625
- w_down: bfloat16 [20480, 7168], P('wide', 'narrow'), may hold values from -0.078125 to 0.078125
- queries: bfloat16 [64, 64, 256], P(('groups', 'wide'), 'narrow'), parts along dimension 0, may hold values from -192 to 192
- new_keys: bfloat16 [64, 256], P(('groups', 'wide')), parts along dimension 0, may hold values from -6 to 6
- new_values: bfloat16 [64, 256], P(('groups', 'wide')), parts along dimension 0, may hold values from -6 to 6
- key_cache: bfloat16 [64, 256, 256], P(('groups', 'wide')), parts along dimension 0, may hold values from -6 to 6
- value_cache: bfloat16 [64, 256, 256], P(('groups', 'wide')), parts along dimension 0, may hold values from -6 to 6
- lengths: int32 [64], P(('groups', 'wide')), parts along dimension 0, may hold values from 1 to 256, as said below
Outputs:
- ffn_out: bfloat16 [96, 7168], P(('groups', 'wide'), 'narrow'), parts along dimension 0
- context: bfloat16 [64, 16384], P(('groups', 'wide'), 'narrow'), parts along dimension 0
There are 2 independent parts, one for each index of `groups`. A program takes and returns all parts, laid end to end along the dimension named above; an argument that names none is the same for every part. Nothing has to cross between parts.
Inputs may be any that keep to these rules, and one draw needn't show every extreme that they name: `routes`: each token names 3 different experts, at most one of them below 4. Among the 6 tokens of one aligned block at most 2 name any one expert below 4; every expert below 4 is named in every block, and one of them is named by exactly 2 tokens of every block. `lengths`: some request of every part has 256.
All inputs are finite; a program needn't handle non-finite values.
Results may differ from a plain program's by a relative error of at most 0.0075.
Values may be sent and summed in bfloat16 or wider, within the bound.
No kernel may reach another device: no remote copies, remote signals or barrier semaphores. Data moves between devices by JAX's collectives and lax.ppermute only.
A program may use at most 128 MiB of HBM per device.

v0:
```python
import jax
import jax.numpy as jnp
from jax import lax
from jax.sharding import PartitionSpec as P

EXPERTS = 4
CAP = 2


def attend(queries, new_keys, new_values, key_cache, value_cache, lengths):
    scaling = queries.shape[-1] ** (-0.5)
    cached = (
        jnp.einsum("rhd,rpd->rhp", queries, key_cache, preferred_element_type=jnp.float32) * scaling
    )
    own_score = (
        jnp.einsum("rhd,rd->rh", queries, new_keys, preferred_element_type=jnp.float32) * scaling
    )
    places = lax.broadcasted_iota(jnp.int32, cached.shape, 2)
    cached = jnp.where(places < lengths[:, None, None], cached, -jnp.inf)
    row_max = jnp.maximum(jnp.max(cached, axis=2), own_score)
    cached_exp = jnp.exp(cached - row_max[:, :, None])
    own_exp = jnp.exp(own_score - row_max)
    denominator = jnp.sum(cached_exp, axis=2) + own_exp
    cached_prob = (cached_exp / denominator[:, :, None]).astype(jnp.bfloat16)
    own_prob = (own_exp / denominator).astype(jnp.bfloat16)
    mixture = jnp.einsum(
        "rhp,rpd->rhd", cached_prob, value_cache, preferred_element_type=jnp.float32
    )
    mixture = (
        mixture
        + own_prob.astype(jnp.float32)[:, :, None] * new_values.astype(jnp.float32)[:, None, :]
    )
    return mixture.astype(jnp.bfloat16).reshape(mixture.shape[0], -1)


def pick_slots(route_rows, expert_ids, capacity):
    named_hits = route_rows == expert_ids[:, None, None]
    hit_mask = jnp.any(named_hits, axis=2)
    slot_rank = jnp.cumsum(hit_mask.astype(jnp.int32), axis=1) - 1
    slot_index = lax.broadcasted_iota(jnp.int32, (1, capacity, 1), 1)
    return (named_hits, hit_mask[:, None, :] & (slot_rank[:, None, :] == slot_index))


def per_device(
    act_rows,
    routes,
    route_weights,
    owners,
    w_gate,
    w_up,
    w_down,
    queries,
    new_keys,
    new_values,
    key_cache,
    value_cache,
    lengths,
):
    devices = lax.axis_size("wide")
    group_size = devices // EXPERTS
    tok_count, half_width = act_rows.shape
    groups_of = lax.broadcasted_iota(jnp.int32, (devices, EXPERTS), 0) // group_size
    owner_cast = (groups_of == owners[None, :]).astype(jnp.bfloat16)
    own_ids = jnp.arange(EXPERTS, dtype=jnp.int32)
    named_hits, slot_picks = pick_slots(
        jnp.broadcast_to(routes[None], (EXPERTS,) + routes.shape), own_ids, CAP
    )
    weight = jnp.sum(jnp.where(named_hits, route_weights[None], 0.0), axis=2)
    every_row, every_route = (
        lax.all_gather(act_rows, "wide", axis=0, tiled=True),
        lax.all_gather(routes, "wide", axis=0, tiled=True),
    )
    my_group = lax.axis_index("wide") // group_size
    my_expert = jnp.sum(jnp.where(owners == my_group, own_ids, 0))
    source_routes = every_route.reshape(devices, tok_count, every_route.shape[1])
    source_ids = jnp.broadcast_to(my_expert, (devices,))
    _, source_picks = pick_slots(source_routes, source_ids, CAP)
    incoming = jnp.einsum(
        "bct,btd->bcd",
        source_picks.astype(jnp.bfloat16),
        every_row.reshape(devices, tok_count, half_width),
        preferred_element_type=jnp.float32,
    ).astype(jnp.bfloat16)
    item_count = incoming.shape[1]
    flattened = incoming.reshape(-1, incoming.shape[2])
    gate_part = jnp.dot(flattened, w_gate, preferred_element_type=jnp.float32)
    up_part = jnp.dot(flattened, w_up, preferred_element_type=jnp.float32)
    gate_sum, up_sum = lax.psum((gate_part, up_part), "narrow")
    hidden = (jax.nn.silu(gate_sum) * up_sum).astype(jnp.bfloat16)
    partial_value = jnp.dot(hidden, w_down, preferred_element_type=jnp.float32).astype(jnp.bfloat16)
    partial_value = partial_value.reshape(incoming.shape[0], item_count, w_down.shape[1])
    returned = lax.all_to_all(partial_value, "wide", split_axis=0, concat_axis=0, tiled=True)
    combined = jnp.einsum("ne,ncd->ecd", owner_cast, returned, preferred_element_type=jnp.float32)
    spread = slot_picks.astype(jnp.float32) * weight[:, None, :]
    ffn_sum = jnp.einsum("ect,ecd->td", spread, combined, precision=lax.Precision.HIGHEST)
    context = attend(queries, new_keys, new_values, key_cache, value_cache, lengths)
    return (ffn_sum.astype(jnp.bfloat16), context)


def solution(mesh):
    in_specs = (
        P(("groups", "wide"), "narrow"),
        P(("groups", "wide"), None),
        P(("groups", "wide"), None),
        P(),
        P("narrow", "wide"),
        P("narrow", "wide"),
        P("wide", "narrow"),
        P(("groups", "wide"), "narrow", None),
        P(("groups", "wide"), None),
        P(("groups", "wide"), None),
        P(("groups", "wide"), None, None),
        P(("groups", "wide"), None, None),
        P(("groups", "wide")),
    )
    out_specs = (P(("groups", "wide"), "narrow"), P(("groups", "wide"), "narrow"))
    return jax.shard_map(
        per_device, mesh=mesh, in_specs=in_specs, out_specs=out_specs, check_vma=False
    )
```

profile of v0, /device:TPU:0, one launch (start us, length us, event | category | flops | bytes accessed | tf_op | source)
XLA Modules:
  0.0 132.3 jit_solution(4025127253607040349)
XLA Ops:
  7.2 0.0 all-reduce.3.cloned.1.call-start
  7.2 28.1 %all-gather = s32[8,6,3]{1,2,0:T(4,128)S(1)} all-gather(s32[1,6,3]{1,2,0:T(4,128)} %bitcast.28), channel_id=1, replica_groups=mesh['groups'=2,'wide'=8,'narrow'=2] {'wide'}, dimensions={0}, use_global_device_ids=true | all-gather | bytes 648 | tf_op jit(solution)/shard_map/all_gather | solution.py:71
  35.3 1.3 fusion.32
  36.6 0.7 compare_reduce_fusion
  37.3 0.2 reduce_window_sum.23
  37.4 31.3 %all-gather.1 = bf16[8,6,3584]{2,1,0:T(8,128)(2,1)S(1)} all-gather(bf16[1,6,3584]{2,1,0:T(8,128)(2,1)} %bitcast.27), channel_id=1, replica_groups=mesh['groups'=2,'wide'=8,'narrow'=2] {'wide'}, dimensions={0}, use_global_device_ids=true | all-gather | bytes 387072 | tf_op jit(solution)/shard_map/all_gather | solution.py:70
  68.7 0.3 convolution_convert_fusion
  69.1 9.5 %fusion.37 = f32[16,2560]{1,0:T(8,128)} fusion(bf16[16,3584]{1,0:T(8,128)(2,1)S(1)} %reshape.51, bf16[3584,2560]{1,0:T(8,128)(2,1)} %param.17), kind=kOutput, calls=%fused_computation.60 | convolution fusion | flops 293601280 | bytes 18628608 | tf_op jit(solution)/shard_map/dot_general | solution.py:86
  78.6 2.0 %copy-done.1 = bf16[3584,2560]{1,0:T(8,128)(2,1)S(1)} copy-done((bf16[3584,2560]{1,0:T(8,128)(2,1)S(1)}, bf16[3584,2560]{1,0:T(8,128)(2,1)}, u32[]{:S(2)}) %copy-start.1) | copy-done | bytes 18350104
  80.6 3.1 %fusion.38 = f32[16,2560]{1,0:T(8,128)} fusion(bf16[16,3584]{1,0:T(8,128)(2,1)S(1)} %reshape.51, bf16[3584,2560]{1,0:T(8,128)(2,1)S(1)} %copy-done.1), kind=kOutput, calls=%fused_computation.61 | convolution fusion | flops 293601280 | bytes 18628608 | tf_op jit(solution)/shard_map/dot_general | solution.py:87
  83.7 0.0 all-reduce.3.cloned.1.call-update
  83.8 0.2 reduce_window_sum.22
  84.0 0.1 fusion.15
  84.1 0.4 fusion.36
  84.5 0.2 fusion.4
  84.7 0.2 fusion.3
  85.0 0.7 copy.23
  85.7 16.0 %all-reduce.3.cloned.1.call-done = (f32[16,2560]{1,0:T(8,128)}, f32[16,2560]{1,0:T(8,128)}) async-done(((f32[16,2560]{1,0:T(8,128)}, f32[16,2560]{1,0:T(8,128)}), (f32[16,2560]{1,0:T(8,128)}, f32[16,2560]{1,0:T(8,128)})) %all-reduce.3.cloned.1.call-update) | async-done | bytes 327696 | tf_op jit(solution)/shard_map/psum | solution.py:88
  101.7 8.9 %convolution_convert_fusion.1 = bf16[16,3584]{1,0:T(8,128)(2,1)S(1)} fusion(bf16[2560,3584]{1,0:T(8,128)(2,1)} %param.19, f32[16,2560]{1,0:T(8,128)} %get-tuple-element.2, f32[16,2560]{1,0:T(8,128)} %get-tuple-element.3), kind=kOutput, calls=%fused_computation.1 | convolution fusion | flops 293904384 | bytes 18792448 | tf_op jit(solution)/shard_map/dot_general | solution.py:90
  110.6 0.7 reshape.52
  111.3 5.8 %all-to-all-start = ((bf16[8,2,3584]{2,1,0:T(2,128)(2,1)}), bf16[8,2,3584]{2,1,0:T(2,128)(2,1)S(1)}, u32[]{:S(2)}, u32[]{:S(2)}) async-start(bf16[8,2,3584]{2,1,0:T(2,128)(2,1)} %reshape.52), calls=%async_computation | async-start | bytes 229376 | tf_op jit(solution)/shard_map/all_to_all | solution.py:92
  117.1 7.2 %all-to-all-done = bf16[8,2,3584]{2,1,0:T(2,128)(2,1)S(1)} async-done(((bf16[8,2,3584]{2,1,0:T(2,128)(2,1)}), bf16[8,2,3584]{2,1,0:T(2,128)(2,1)S(1)}, u32[]{:S(2)}, u32[]{:S(2)}) %all-to-all-start) | async-done | bytes 114720 | tf_op jit(solution)/shard_map/all_to_all | solution.py:92
  124.3 0.2 fusion.5
  124.5 0.9 fusion
  (31 shorter events, 0.2 us)
Async XLA Ops:
  7.2 77.0 %copy-start = (bf16[4,256,256]{2,1,0:T(8,128)(2,1)S(1)}, bf16[4,256,256]{2,1,0:T(8,128)(2,1)}, u32[]{:S(2)}) copy-start(bf16[4,256,256]{2,1,0:T(8,128)(2,1)} %param.23) | copy-start | bytes 1572868
  7.2 94.5 %all-reduce.3.cloned.1.call-start = ((), (), s32[]{:S(2)}) async-start(), calls=%async_computation.1 | async-start | bytes 655360 | tf_op jit(solution)/shard_map/psum | solution.py:88
  69.1 11.5 %copy-start.1 = (bf16[3584,2560]{1,0:T(8,128)(2,1)S(1)}, bf16[3584,2560]{1,0:T(8,128)(2,1)}, u32[]{:S(2)}) copy-start(bf16[3584,2560]{1,0:T(8,128)(2,1)} %param.18) | copy-start | bytes 55050244
  80.6 3.2 %copy-start.3 = (s32[6,3]{0,1:T(4,128)S(1)}, s32[6,3]{0,1:T(4,128)}, u32[]{:S(2)}) copy-start(s32[6,3]{0,1:T(4,128)} %param.14) | copy-start | bytes 220
  80.6 3.4 %copy-start.2 = (bf16[4,32,256]{2,1,0:T(8,128)(2,1)S(1)}, bf16[4,32,256]{2,1,0:T(8,128)(2,1)}, u32[]{:S(2)}) copy-start(bf16[4,32,256]{2,1,0:T(8,128)(2,1)} %param.20) | copy-start | bytes 196612
  80.6 3.4 %copy-start.9 = (bf16[4,256]{1,0:T(4,128)(2,1)S(1)}, bf16[4,256]{1,0:T(4,128)(2,1)}, u32[]{:S(2)}) copy-start(bf16[4,256]{1,0:T(4,128)(2,1)} %param.21) | copy-start | bytes 6148
  80.6 3.6 %copy-start.6 = (s32[4]{0:T(128)S(1)}, s32[4]{0:T(128)}, u32[]{:S(2)}) copy-start(s32[4]{0:T(128)} %param.25) | copy-start | bytes 52
  80.6 4.1 %copy-start.4 = (bf16[4,256]{1,0:T(4,128)(2,1)S(1)}, bf16[4,256]{1,0:T(4,128)(2,1)}, u32[]{:S(2)}) copy-start(bf16[4,256]{1,0:T(4,128)(2,1)} %param.22) | copy-start | bytes 6148
  80.6 4.1 %copy-start.8 = (bf16[4,256,256]{2,1,0:T(8,128)(2,1)S(1)}, bf16[4,256,256]{2,1,0:T(8,128)(2,1)}, u32[]{:S(2)}) copy-start(bf16[4,256,256]{2,1,0:T(8,128)(2,1)} %param.24) | copy-start | bytes 1572868
  80.6 5.1 %copy-start.5 = (f32[6,3]{0,1:T(4,128)S(1)}, f32[6,3]{0,1:T(4,128)}, u32[]{:S(2)}) copy-start(f32[6,3]{0,1:T(4,128)} %param.15) | copy-start | bytes 220
  83.7 40.5 %copy-start.7 = (s32[4]{0:T(128)S(1)}, s32[4]{0:T(128)}, u32[]{:S(2)}) copy-start(s32[4]{0:T(128)} %param.16) | copy-start | bytes 52
  111.3 13.0 %all-to-all-start = ((bf16[8,2,3584]{2,1,0:T(2,128)(2,1)}), bf16[8,2,3584]{2,1,0:T(2,128)(2,1)S(1)}, u32[]{:S(2)}, u32[]{:S(2)}) async-start(bf16[8,2,3584]{2,1,0:T(2,128)(2,1)} %reshape.52), calls=%async_computation | async-start | bytes 229376 | tf_op jit(solution)/shard_map/all_to_all | solution.py:92
Sparse Core Ops, SparseCore 0:
  83.9 17.7 all-reduce.2
where the time goes:
time: 133 us; the launch traced here: 132 us
  blocking collectives  59.4 us (45%)
  matrix products  23.7 us (18%)
  waiting for transfers between devices  23.3 us (18%)
  between operations  14.2 us (11%)
  starting transfers between devices  5.81 us (4%)
  local copies, waits for them, and re-layouts  3.47 us (3%)
  other arithmetic  2.56 us (2%)
    all_gather x1, blocking collectives, per_device(): lax.all_gather(act_rows, 'wide', axis=0, tiled=True)  31.3 us
    all_gather x1, blocking collectives, per_device(): lax.all_gather(routes, 'wide', axis=0, tiled=True)  28.1 us
    psum x1, waiting for transfers between devices, per_device(): gate_sum, up_sum = lax.psum((gate_part, up_part), 'narrow')  16 us
    dot_general x1, matrix products, per_device(): gate_part = jnp.dot(flattened, w_gate, preferred_element_type=jnp.float32)  9.51 us
    dot_general x1, matrix products, per_device(): jnp.dot(hidden, w_down, preferred_element_type=jnp.float32)  8.88 us
    all_to_all x1, waiting for transfers between devices, per_device(): lax.all_to_all(partial_value, 'wide', split_axis=0, concat_axis=0, tiled=...  7.23 us
    all_to_all x1, starting transfers between devices, per_device(): lax.all_to_all(partial_value, 'wide', split_axis=0, concat_axis=0, tiled=...  5.77 us
    dot_general x1, matrix products, per_device(): up_part = jnp.dot(flattened, w_up, preferred_element_type=jnp.float32)  3.14 us
  transfers between devices with their start and end apart: 2, of which 2 were waited for; matrix products, arithmetic and copies ran while one was open for 1% of the time, Pallas kernels for 0%

commit v1 on v0

v1 whole, which is shorter than its diff:
```python
import functools

import jax
import jax.numpy as jnp
from jax import lax
from jax.experimental import pallas as pl
from jax.experimental.pallas import tpu as pltpu
from jax.sharding import PartitionSpec as P

EXPERTS = 4
CAP = 2
SLOTS = EXPERTS * CAP
F32 = jnp.float32
BF16 = jnp.bfloat16

VMEM = pl.BlockSpec(memory_space=pltpu.VMEM)
SMEM = pl.BlockSpec(memory_space=pltpu.SMEM)


def params(mib):
    return pltpu.CompilerParams(vmem_limit_bytes=mib * 1024 * 1024)


def expert_of(owners_ref, block):
    found = jnp.int32(0)
    for expert in range(EXPERTS):
        found += jnp.where(owners_ref[expert] == block, expert, 0)
    return found


def slot_experts(owners_ref, base, iota):
    ids = jnp.zeros_like(iota)
    for m in range(EXPERTS):
        ids = jnp.where(iota // CAP == m, expert_of(owners_ref, base ^ m), ids)
    return ids


def pick_kernel(group_size, owners_ref, routes_ref, act_ref, out_ref):
    tokens = act_ref.shape[0]
    here = lax.axis_index("wide") // group_size
    rows = lax.broadcasted_iota(jnp.int32, (SLOTS, tokens), 0)
    cols = lax.broadcasted_iota(jnp.int32, (SLOTS, tokens), 1)
    ids = slot_experts(owners_ref, here, rows)
    hit = jnp.zeros((SLOTS, tokens), F32)
    for k in range(routes_ref.shape[0]):
        hit = jnp.where(routes_ref[k : k + 1, :] == ids, 1.0, hit)
    rank = jnp.zeros((SLOTS, tokens), F32)
    for t in range(tokens - 1):
        rank += jnp.where(cols > t, hit[:, t : t + 1], 0.0)
    picks = jnp.where(rank == (rows % CAP).astype(F32), hit, 0.0).astype(BF16)
    out_ref[...] = jnp.dot(picks, act_ref[...], preferred_element_type=F32).astype(BF16)


def pick_rows(owners, routes_t, act_rows, group_size):
    return pl.pallas_call(
        functools.partial(pick_kernel, group_size),
        out_shape=jax.ShapeDtypeStruct((SLOTS, act_rows.shape[1]), BF16),
        in_specs=[SMEM, VMEM, VMEM],
        out_specs=VMEM,
        compiler_params=params(4),
        name="pick_rows",
    )(owners, routes_t, act_rows)


def message_kernel(near_ref, far_ref, *out_refs):
    pieces = [ref[j].astype(F32) for ref in (near_ref, far_ref) for j in range(ref.shape[0])]
    for m, out_ref in enumerate(out_refs):
        chosen = [piece[m * CAP : (m + 1) * CAP] for piece in pieces]
        out_ref[...] = jnp.concatenate(chosen, axis=0).astype(BF16)


def messages(near, far):
    rows = CAP * (near.shape[0] + far.shape[0])
    shape = jax.ShapeDtypeStruct((rows, near.shape[2]), BF16)
    return pl.pallas_call(
        message_kernel,
        out_shape=(shape,) * EXPERTS,
        in_specs=[VMEM, VMEM],
        out_specs=(VMEM,) * EXPERTS,
        compiler_params=params(16),
        name="messages",
    )(near, far)


def gate_up_kernel(depth, *refs):
    msg_refs = refs[:EXPERTS]
    gate_ref, up_ref, gate_out, up_out, rows_ref = refs[EXPERTS:]
    step = pl.program_id(0)

    @pl.when(step == 0)
    def _():
        rows = jnp.concatenate([ref[...].astype(F32) for ref in msg_refs], axis=0).astype(BF16)
        for k in range(rows_ref.shape[0]):
            rows_ref[k] = rows[:, k * depth : (k + 1) * depth]
        gate_out[...] = jnp.zeros_like(gate_out)
        up_out[...] = jnp.zeros_like(up_out)

    rows = rows_ref[step]
    gate_out[...] += jnp.dot(rows, gate_ref[...], preferred_element_type=F32)
    up_out[...] += jnp.dot(rows, up_ref[...], preferred_element_type=F32)


def gate_up(msgs, w_gate, w_up, depth=256):
    features, hidden = w_gate.shape
    rows = sum(m.shape[0] for m in msgs)
    shape = jax.ShapeDtypeStruct((rows, hidden), F32)
    whole = [pl.BlockSpec(m.shape, lambda k: (0, 0)) for m in msgs]
    weight = pl.BlockSpec((depth, hidden), lambda k: (k, 0))
    out = pl.BlockSpec((rows, hidden), lambda k: (0, 0))
    return pl.pallas_call(
        functools.partial(gate_up_kernel, depth),
        out_shape=(shape, shape),
        grid=(features // depth,),
        in_specs=whole + [weight, weight],
        out_specs=(out, out),
        scratch_shapes=[pltpu.VMEM((features // depth, rows, depth), BF16)],
        compiler_params=params(40),
        name="gate_up",
    )(*msgs, w_gate, w_up)


def down_kernel(group_size, depth, ga, gb, ua, ub, down_ref, out_ref, hid_ref, acc_ref):
    step = pl.program_id(0)
    steps = hid_ref.shape[0]

    @pl.when(step == 0)
    def _():
        gate = ga[...] + gb[...]
        up = ua[...] + ub[...]
        hidden = (gate / (1.0 + jnp.exp(-gate)) * up).astype(BF16)
        for k in range(steps):
            hid_ref[k] = hidden[:, k * depth : (k + 1) * depth]
        acc_ref[...] = jnp.zeros_like(acc_ref)

    acc_ref[...] += jnp.dot(hid_ref[step], down_ref[...], preferred_element_type=F32)

    @pl.when(step == steps - 1)
    def _():
        wide = lax.axis_index("wide")
        block, place = wide // group_size, wide % group_size
        acc = acc_ref[...]
        for m in range(EXPERTS):
            for j in range(group_size):
                target = (block ^ m) * group_size + (place ^ j)
                start = (m * group_size + j) * CAP
                out_ref[target] = acc[start : start + CAP].astype(BF16)


def down(gate_pair, up_pair, w_down, group_size, depth):
    hidden, features = w_down.shape
    rows = gate_pair[0].shape[0]
    devices = rows // CAP
    whole = pl.BlockSpec((rows, hidden), lambda k: (0, 0))
    return pl.pallas_call(
        functools.partial(down_kernel, group_size, depth),
        out_shape=jax.ShapeDtypeStruct((devices, CAP, features), BF16),
        grid=(hidden // depth,),
        in_specs=[whole] * 4 + [pl.BlockSpec((depth, features), lambda k: (k, 0))],
        out_specs=pl.BlockSpec((devices, CAP, features), lambda k: (0, 0, 0)),
        scratch_shapes=[
            pltpu.VMEM((hidden // depth, rows, depth), BF16),
            pltpu.VMEM((rows, features), F32),
        ],
        compiler_params=params(40),
        name="down",
    )(*gate_pair, *up_pair, w_down)


def combine_kernel(group_size, owners_ref, routes_ref, weights_ref, back_ref, out_ref, rows_ref):
    tokens = out_ref.shape[0]
    devices = back_ref.shape[0]
    for d in range(devices):
        rows_ref[d * CAP : (d + 1) * CAP, :] = back_ref[d].astype(F32)
    eye = lax.broadcasted_iota(jnp.int32, (tokens, tokens), 0) == lax.broadcasted_iota(
        jnp.int32, (tokens, tokens), 1
    )
    width = devices * CAP
    rows = lax.broadcasted_iota(jnp.int32, (tokens, width), 0)
    slot = lax.broadcasted_iota(jnp.int32, (tokens, width), 1)
    block = slot // (CAP * group_size)
    ids = jnp.zeros_like(slot)
    for b in range(EXPERTS):
        ids = jnp.where(block == b, expert_of(owners_ref, b), ids)
    hit = jnp.zeros((tokens, width), F32)
    weight = jnp.zeros((tokens, 1), F32)
    for k in range(routes_ref.shape[0]):
        named = jnp.where(eye, routes_ref[k : k + 1, :], 0).sum(axis=1, keepdims=True)
        given = jnp.where(eye, weights_ref[k : k + 1, :], 0.0).sum(axis=1, keepdims=True)
        hit = jnp.where(named == ids, 1.0, hit)
        weight += jnp.where(named < EXPERTS, given, 0.0)
    rank = jnp.zeros((tokens, width), F32)
    for t in range(tokens - 1):
        rank += jnp.where(rows > t, hit[t : t + 1, :], 0.0)
    picks = jnp.where(rank == (slot % CAP).astype(F32), hit, 0.0).astype(BF16)
    total = jnp.dot(picks, rows_ref[...].astype(BF16), preferred_element_type=F32)
    out_ref[...] = (weight * total).astype(BF16)


def combine(owners, routes_t, weights_t, back, group_size):
    devices, _, features = back.shape
    return pl.pallas_call(
        functools.partial(combine_kernel, group_size),
        out_shape=jax.ShapeDtypeStruct((routes_t.shape[1], features), BF16),
        in_specs=[SMEM, VMEM, VMEM, VMEM],
        out_specs=VMEM,
        scratch_shapes=[pltpu.VMEM((devices * CAP, features), F32)],
        compiler_params=params(16),
        name="combine",
    )(owners, routes_t, weights_t, back)


def attend_kernel(lengths_ref, q_ref, nk_ref, nv_ref, keys_ref, values_ref, out_ref, turn_ref):
    requests, heads, size = q_ref.shape
    scaling = size ** (-0.5)
    for r in range(requests):
        q = q_ref[r]
        score = lax.dot_general(
            q, keys_ref[r], (((1,), (1,)), ((), ())), preferred_element_type=F32
        )
        score = score * scaling
        own = jnp.sum(q.astype(F32) * nk_ref[r : r + 1, :].astype(F32), axis=1, keepdims=True)
        own = own * scaling
        place = lax.broadcasted_iota(jnp.int32, score.shape, 1)
        score = jnp.where(place < lengths_ref[r], score, -jnp.inf)
        top = jnp.maximum(jnp.max(score, axis=1, keepdims=True), own)
        score = jnp.exp(score - top)
        own = jnp.exp(own - top)
        total = jnp.sum(score, axis=1, keepdims=True) + own
        prob = (score / total).astype(BF16)
        own = (own / total).astype(BF16).astype(F32)
        mixed = jnp.dot(prob, values_ref[r], preferred_element_type=F32)
        turn_ref[:, r, :] = mixed + own * nv_ref[r : r + 1, :].astype(F32)
    for h in range(heads):
        out_ref[:, h * size : (h + 1) * size] = turn_ref[h].astype(BF16)


def attend(queries, new_keys, new_values, key_cache, value_cache, lengths):
    requests, heads, size = queries.shape
    return pl.pallas_call(
        attend_kernel,
        out_shape=jax.ShapeDtypeStruct((requests, heads * size), BF16),
        in_specs=[SMEM] + [VMEM] * 5,
        out_specs=VMEM,
        scratch_shapes=[pltpu.VMEM((heads, requests, size), F32)],
        compiler_params=params(8),
        name="attend",
    )(lengths, queries, new_keys, new_values, key_cache, value_cache)


def swap(x, axis, devices, mask):
    return lax.ppermute(x, axis, [(i, i ^ mask) for i in range(devices)])


def per_device(
    act_rows,
    routes,
    route_weights,
    owners,
    w_gate,
    w_up,
    w_down,
    queries,
    new_keys,
    new_values,
    key_cache,
    value_cache,
    lengths,
):
    devices = lax.axis_size("wide")
    group_size = devices // EXPERTS
    routes_t, weights_t = routes.T, route_weights.T
    near = pick_rows(owners, routes_t, act_rows, group_size)[None]
    mask = 1
    while 2 * mask < group_size:
        near = jnp.concatenate([near, swap(near, "wide", devices, mask)], axis=0)
        mask *= 2
    far = swap(near, "wide", devices, mask)
    msgs = list(messages(near, far))
    for m in range(1, EXPERTS):
        msgs[m] = swap(msgs[m], "wide", devices, m * group_size)
    context = attend(queries, new_keys, new_values, key_cache, value_cache, lengths)
    gate, up = gate_up(msgs, w_gate, w_up)
    gate_pair = (gate, swap(gate, "narrow", 2, 1))
    up_pair = (up, swap(up, "narrow", 2, 1))
    depth = min(256, w_down.shape[0])
    if w_down.shape[0] % depth:
        depth = w_down.shape[0]
    partial_value = down(gate_pair, up_pair, w_down, group_size, depth)
    back = lax.all_to_all(partial_value, "wide", split_axis=0, concat_axis=0, tiled=True)
    ffn_out = combine(owners, routes_t, weights_t, back, group_size)
    return (ffn_out, context)


def solution(mesh):
    in_specs = (
        P(("groups", "wide"), "narrow"),
        P(("groups", "wide"), None),
        P(("groups", "wide"), None),
        P(),
        P("narrow", "wide"),
        P("narrow", "wide"),
        P("wide", "narrow"),
        P(("groups", "wide"), "narrow", None),
        P(("groups", "wide"), None),
        P(("groups", "wide"), None),
        P(("groups", "wide"), None, None),
        P(("groups", "wide"), None, None),
        P(("groups", "wide")),
    )
    out_specs = (P(("groups", "wide"), "narrow"), P(("groups", "wide"), "narrow"))
    return jax.shard_map(
        per_device, mesh=mesh, in_specs=in_specs, out_specs=out_specs, check_vma=False
    )
```

time: 133 us -> 61.9 us (0.47)
  blocking collectives: 59.4 us -> 0 us
  Pallas kernels: 0 us -> 33.3 us
  matrix products: 23.7 us -> 0 us
  between operations: 14.2 us -> 0.79 us
  waiting for transfers between devices: 23.3 us -> 13.4 us
  starting transfers between devices: 5.81 us -> 11.7 us
  other arithmetic: 2.56 us -> 0 us
    all_gather x2 -> x0, blocking collectives: 59.4 us -> none  [the longest x1 31.3 us: per_device(): lax.all_gather(act_rows, 'wide', axis=0, tiled=True)]
    pallas_call x0 -> x6, Pallas kernels: none -> 33.3 us  [the longest x1 17.1 us: gate_up(): pl.pallas_call(functools.partial(gate_up_kernel, depth), out_shape=(shape...]
    dot_general x9 -> x0, matrix products: 23.7 us -> none  [the longest x1 9.51 us: per_device(): gate_part = jnp.dot(flattened, w_gate, preferred_element_type=jnp.float32)]
    psum x1 -> x0, waiting for transfers between devices: 16 us -> none  [per_device(): gate_sum, up_sum = lax.psum((gate_part, up_part), 'narrow')]
    ppermute x0 -> x6, waiting for transfers between devices: none -> 8.94 us  [swap(): return lax.ppermute(x, axis, [(i, i ^ mask) for i in range(devices)])]
    ppermute x0 -> x6, starting transfers between devices: none -> 8.33 us  [swap(): return lax.ppermute(x, axis, [(i, i ^ mask) for i in range(devices)])]
    all_to_all x1, waiting for transfers between devices: 7.23 us -> 4.51 us  [per_device(): lax.all_to_all(partial_value, 'wide', split_axis=0, concat_axis=0, tiled=...]
    all_to_all x1, starting transfers between devices: 5.77 us -> 3.37 us  [per_device(): lax.all_to_all(partial_value, 'wide', split_axis=0, concat_axis=0, tiled=...]
  transfers between devices with their start and end apart: 2 -> 7, of which waited for: 2 -> 6; matrix products, arithmetic and copies ran while one was open for 1% -> 0% of each run, Pallas kernels for 0% -> 5%
where the time goes in v1:
time: 61.9 us; the launch traced here: 61.4 us
  Pallas kernels  33.3 us (54%)
  waiting for transfers between devices  13.4 us (22%)
  starting transfers between devices  11.7 us (19%)
  local copies, waits for them, and re-layouts  2.21 us (4%)
  between operations  0.79 us (1%)
    pallas_call x1, Pallas kernels, gate_up(): pl.pallas_call(functools.partial(gate_up_kernel, depth), out_shape=(shape...  17.1 us
    pallas_call x1, Pallas kernels, down(): pl.pallas_call(functools.partial(down_kernel, group_size, depth), out_sha...  11.1 us
    ppermute x6, waiting for transfers between devices, swap(): return lax.ppermute(x, axis, [(i, i ^ mask) for i in range(devices)])  8.94 us
    ppermute x6, starting transfers between devices, swap(): return lax.ppermute(x, axis, [(i, i ^ mask) for i in range(devices)])  8.33 us
    all_to_all x1, waiting for transfers between devices, per_device(): lax.all_to_all(partial_value, 'wide', split_axis=0, concat_axis=0, tiled=...  4.51 us
    all_to_all x1, starting transfers between devices, per_device(): lax.all_to_all(partial_value, 'wide', split_axis=0, concat_axis=0, tiled=...  3.37 us
    pallas_call x1, Pallas kernels, attend(): pl.pallas_call(attend_kernel, out_shape=jax.ShapeDtypeStruct((requests, h...  2.83 us
    unnamed x24, local copies, waits for them, and re-layouts  2.21 us
  transfers between devices with their start and end apart: 7, of which 6 were waited for; matrix products, arithmetic and copies ran while one was open for 0% of the time, Pallas kernels for 5%

profile of v1, /device:TPU:0, one launch (start us, length us, event | category | flops | bytes accessed | tf_op | source)
XLA Modules:
  0.0 61.4 jit_solution(16386975723037703112)
XLA Ops:
  0.6 0.8 %copy-done.3 = bf16[6,3584]{1,0:T(8,128)(2,1)S(1)} copy-done((bf16[6,3584]{1,0:T(8,128)(2,1)S(1)}, bf16[6,3584]{1,0:T(8,128)(2,1)}, u32[]{:S(2)}) %copy-start.3) | copy-done | bytes 43032
  1.5 0.7 %copy-done.4 = s32[6,3]{0,1:T(4,128)S(1)} copy-done((s32[6,3]{0,1:T(4,128)S(1)}, s32[6,3]{0,1:T(4,128)}, u32[]{:S(2)}) %copy-start.4) | copy-done | bytes 96
  2.1 0.7 %copy-done.9 = s32[4]{0:T(128)S(1)} copy-done((s32[4]{0:T(128)S(1)}, s32[4]{0:T(128)}, u32[]{:S(2)}) %copy-start.9) | copy-done | bytes 40
  2.8 0.8 %pick_rows.1 = bf16[8,3584]{1,0:T(8,128)(2,1)S(1)} custom-call(s32[4]{0:T(128)S(1)} %copy-done.9, s32[3,6]{1,0:T(4,128)S(1)} %bitcast.5, bf16[6,3584]{1,0:T(8,128)(2,1)S(1)} %copy-done.3), custom_call_target="tpu_custom_call" | custom-call | tf_op jit(solution)/shard_map/pick_rows/pallas_call | solution.py:55
  3.6 3.0 %collective-permute-start = (bf16[1,8,3584]{2,1,0:T(8,128)(2,1)S(1)}, bf16[1,8,3584]{2,1,0:T(8,128)(2,1)S(1)}, u32[]{:S(2)}, u32[]{:S(2)}) collective-permute-start(bf16[1,8,3584]{2,1,0:T(8,128)(2,1)S(1)} %bitcast.3), channel_id=1, source_target_pairs={{0,2},{2,0},{4,6},{6,4},{8,10},{10,8},{12,14},{14,12},{1,3},{3,1},... | collective-permute-start | bytes 172040 | tf_op jit(solution)/shard_map/ppermute | solution.py:251
  6.6 2.2 %collective-permute-done.far_ref = bf16[1,8,3584]{2,1,0:T(8,128)(2,1)S(1)} collective-permute-done((bf16[1,8,3584]{2,1,0:T(8,128)(2,1)S(1)}, bf16[1,8,3584]{2,1,0:T(8,128)(2,1)S(1)}, u32[]{:S(2)}, u32[]{:S(2)}) %collective-permute-start) | collective-permute-done | bytes 57376 | tf_op jit(solution)/shard_map/ppermute | solution.py:251
  8.7 0.1 messages.1
  8.8 2.2 %collective-permute-start.1 = (bf16[4,3584]{1,0:T(4,128)(2,1)S(1)}, bf16[4,3584]{1,0:T(4,128)(2,1)S(1)}, u32[]{:S(2)}, u32[]{:S(2)}) collective-permute-start(bf16[4,3584]{1,0:T(4,128)(2,1)S(1)} %get-tuple-element.9), channel_id=1, source_target_pairs={{0,4},{2,6},{4,0},{6,2},{8,12},{10,14},{12,8},{14,10},{1,5},{3,7},... | collective-permute-start | bytes 86024 | tf_op jit(solution)/shard_map/ppermute | solution.py:251
  11.0 2.6 %collective-permute-start.2 = (bf16[4,3584]{1,0:T(4,128)(2,1)S(1)}, bf16[4,3584]{1,0:T(4,128)(2,1)S(1)}, u32[]{:S(2)}, u32[]{:S(2)}) collective-permute-start(bf16[4,3584]{1,0:T(4,128)(2,1)S(1)} %get-tuple-element.10), channel_id=1, source_target_pairs={{0,8},{2,10},{4,12},{6,14},{8,0},{10,2},{12,4},{14,6},{1,9},{3,11}... | collective-permute-start | bytes 86024 | tf_op jit(solution)/shard_map/ppermute | solution.py:251
  13.6 2.3 %collective-permute-done.2.refs_2_ = bf16[4,3584]{1,0:T(4,128)(2,1)S(1)} collective-permute-done((bf16[4,3584]{1,0:T(4,128)(2,1)S(1)}, bf16[4,3584]{1,0:T(4,128)(2,1)S(1)}, u32[]{:S(2)}, u32[]{:S(2)}) %collective-permute-start.2) | collective-permute-done | bytes 28704 | tf_op jit(solution)/shard_map/ppermute | solution.py:251
  15.9 3.3 %collective-permute-done.3.refs_3_ = bf16[4,3584]{1,0:T(4,128)(2,1)S(1)} collective-permute-done((bf16[4,3584]{1,0:T(4,128)(2,1)S(1)}, bf16[4,3584]{1,0:T(4,128)(2,1)S(1)}, u32[]{:S(2)}, u32[]{:S(2)}) %collective-permute-start.3) | collective-permute-done | bytes 28704 | tf_op jit(solution)/shard_map/ppermute | solution.py:251
  19.2 17.1 %gate_up.1 = (f32[16,2560]{1,0:T(8,128)S(1)}, f32[16,2560]{1,0:T(8,128)S(1)}) custom-call(bf16[4,3584]{1,0:T(4,128)(2,1)S(1)} %get-tuple-element.8.refs_0_, bf16[4,3584]{1,0:T(4,128)(2,1)S(1)} %collective-permute-done.1.refs_1_, bf16[4,3584]{1,0:T(4,128)(2,1)S(1)} %collective-permute-done.2.refs_2_, bf16[4,3584]{1,0:T(4,128)(2,1)S(1)} %collective-permute-done.3.refs_3_, ...), custom_call_target="tpu_custom_call" | custom-call | tf_op jit(solution)/shard_map/gate_up/pallas_call | solution.py:110
  36.3 0.0 copy-start.1
  36.4 0.0 copy-start.7
  36.4 0.0 copy-start.11
  36.4 0.1 collective-permute-start.4
  36.5 0.5 collective-permute-start.5
  37.0 0.9 %collective-permute-done.4.gb = f32[16,2560]{1,0:T(8,128)S(1)} collective-permute-done((f32[16,2560]{1,0:T(8,128)S(1)}, f32[16,2560]{1,0:T(8,128)S(1)}, u32[]{:S(2)}, u32[]{:S(2)}) %collective-permute-start.4) | collective-permute-done | bytes 163872 | tf_op jit(solution)/shard_map/ppermute | solution.py:251
  37.9 0.2 collective-permute-done.5.ub
  38.1 11.1 %down.1 = bf16[8,2,3584]{2,1,0:T(2,128)(2,1)} custom-call(f32[16,2560]{1,0:T(8,128)S(1)} %get-tuple-element.12.ga, f32[16,2560]{1,0:T(8,128)S(1)} %collective-permute-done.4.gb, f32[16,2560]{1,0:T(8,128)S(1)} %get-tuple-element.13.ua, f32[16,2560]{1,0:T(8,128)S(1)} %collective-permute-done.5.ub, bf16[2560,3584]{1,0:T(8,128)(2,1)} %down_ref.1), custom_call_target="tpu_custom_call" | custom-call | tf_op jit(solution)/shard_map/down/pallas_call | solution.py:154
  49.2 3.4 %all-to-all-start = ((bf16[8,2,3584]{2,1,0:T(2,128)(2,1)}), bf16[8,2,3584]{2,1,0:T(2,128)(2,1)S(1)}, u32[]{:S(2)}, u32[]{:S(2)}) async-start(bf16[8,2,3584]{2,1,0:T(2,128)(2,1)} %down.1), calls=%async_computation | async-start | bytes 229376 | tf_op jit(solution)/shard_map/all_to_all | solution.py:289
  52.6 2.8 %attend.1 = bf16[4,8192]{1,0:T(4,128)(2,1)} custom-call(s32[4]{0:T(128)S(1)} %copy-done.11, bf16[4,32,256]{2,1,0:T(8,128)(2,1)S(1)} %copy-done.2, bf16[4,256]{1,0:T(4,128)(2,1)S(1)} %copy-done.6, bf16[4,256]{1,0:T(4,128)(2,1)S(1)} %copy-done.7, bf16[4,256,256]{2,1,0:T(8,128)(2,1)S(1)} %copy-done, bf16[4,256,256]{2,1,0:T(8,128)(2,1)S(1)} %copy-done.1), custom_call_target="tpu_custom_call" | custom-call | tf_op jit(solution)/shard_map/attend/pallas_call | solution.py:239
  55.5 4.5 %all-to-all-done.back_ref = bf16[8,2,3584]{2,1,0:T(2,128)(2,1)S(1)} async-done(((bf16[8,2,3584]{2,1,0:T(2,128)(2,1)}), bf16[8,2,3584]{2,1,0:T(2,128)(2,1)S(1)}, u32[]{:S(2)}, u32[]{:S(2)}) %all-to-all-start) | async-done | bytes 114720 | tf_op jit(solution)/shard_map/all_to_all | solution.py:289
  60.0 1.4 %combine.1 = bf16[6,3584]{1,0:T(8,128)(2,1)} custom-call(s32[4]{0:T(128)S(1)} %copy-done.10, s32[3,6]{1,0:T(4,128)S(1)} %bitcast.6, f32[3,6]{1,0:T(4,128)S(1)} %bitcast.7, bf16[8,2,3584]{2,1,0:T(2,128)(2,1)S(1)} %all-to-all-done.back_ref), custom_call_target="tpu_custom_call" | custom-call | tf_op jit(solution)/shard_map/combine/pallas_call | solution.py:201
  (20 shorter events, 0.1 us)
Async XLA Ops:
  0.6 0.8 %copy-start.3 = (bf16[6,3584]{1,0:T(8,128)(2,1)S(1)}, bf16[6,3584]{1,0:T(8,128)(2,1)}, u32[]{:S(2)}) copy-start(bf16[6,3584]{1,0:T(8,128)(2,1)} %act_ref.1) | copy-start | bytes 129028
  1.4 0.7 %copy-start.4 = (s32[6,3]{0,1:T(4,128)S(1)}, s32[6,3]{0,1:T(4,128)}, u32[]{:S(2)}) copy-start(s32[6,3]{0,1:T(4,128)} %param.14) | copy-start | bytes 220
  2.1 0.7 %copy-start.9 = (s32[4]{0:T(128)S(1)}, s32[4]{0:T(128)}, u32[]{:S(2)}) copy-start(s32[4]{0:T(128)} %owners_ref.3) | copy-start | bytes 52
  3.6 5.2 %collective-permute-start = (bf16[1,8,3584]{2,1,0:T(8,128)(2,1)S(1)}, bf16[1,8,3584]{2,1,0:T(8,128)(2,1)S(1)}, u32[]{:S(2)}, u32[]{:S(2)}) collective-permute-start(bf16[1,8,3584]{2,1,0:T(8,128)(2,1)S(1)} %bitcast.3), channel_id=1, source_target_pairs={{0,2},{2,0},{4,6},{6,4},{8,10},{10,8},{12,14},{14,12},{1,3},{3,1},... | collective-permute-start | bytes 172040 | tf_op jit(solution)/shard_map/ppermute | solution.py:251
  8.8 4.8 %collective-permute-start.1 = (bf16[4,3584]{1,0:T(4,128)(2,1)S(1)}, bf16[4,3584]{1,0:T(4,128)(2,1)S(1)}, u32[]{:S(2)}, u32[]{:S(2)}) collective-permute-start(bf16[4,3584]{1,0:T(4,128)(2,1)S(1)} %get-tuple-element.9), channel_id=1, source_target_pairs={{0,4},{2,6},{4,0},{6,2},{8,12},{10,14},{12,8},{14,10},{1,5},{3,7},... | collective-permute-start | bytes 86024 | tf_op jit(solution)/shard_map/ppermute | solution.py:251
  11.0 4.9 %collective-permute-start.2 = (bf16[4,3584]{1,0:T(4,128)(2,1)S(1)}, bf16[4,3584]{1,0:T(4,128)(2,1)S(1)}, u32[]{:S(2)}, u32[]{:S(2)}) collective-permute-start(bf16[4,3584]{1,0:T(4,128)(2,1)S(1)} %get-tuple-element.10), channel_id=1, source_target_pairs={{0,8},{2,10},{4,12},{6,14},{8,0},{10,2},{12,4},{14,6},{1,9},{3,11}... | collective-permute-start | bytes 86024 | tf_op jit(solution)/shard_map/ppermute | solution.py:251
  13.6 5.7 %collective-permute-start.3 = (bf16[4,3584]{1,0:T(4,128)(2,1)S(1)}, bf16[4,3584]{1,0:T(4,128)(2,1)S(1)}, u32[]{:S(2)}, u32[]{:S(2)}) collective-permute-start(bf16[4,3584]{1,0:T(4,128)(2,1)S(1)} %get-tuple-element.11), channel_id=1, source_target_pairs={{0,12},{2,14},{4,8},{6,10},{8,4},{10,6},{12,0},{14,2},{1,13},{3,15... | collective-permute-start | bytes 86024 | tf_op jit(solution)/shard_map/ppermute | solution.py:251
  36.3 16.3 %copy-start = (bf16[4,256,256]{2,1,0:T(8,128)(2,1)S(1)}, bf16[4,256,256]{2,1,0:T(8,128)(2,1)}, u32[]{:S(2)}) copy-start(bf16[4,256,256]{2,1,0:T(8,128)(2,1)} %keys_ref.1) | copy-start | bytes 1572868
  36.3 16.3 %copy-start.1 = (bf16[4,256,256]{2,1,0:T(8,128)(2,1)S(1)}, bf16[4,256,256]{2,1,0:T(8,128)(2,1)}, u32[]{:S(2)}) copy-start(bf16[4,256,256]{2,1,0:T(8,128)(2,1)} %values_ref.1) | copy-start | bytes 1572868
  36.4 16.3 %copy-start.2 = (bf16[4,32,256]{2,1,0:T(8,128)(2,1)S(1)}, bf16[4,32,256]{2,1,0:T(8,128)(2,1)}, u32[]{:S(2)}) copy-start(bf16[4,32,256]{2,1,0:T(8,128)(2,1)} %q_ref.1) | copy-start | bytes 196612
  36.4 16.2 %copy-start.6 = (bf16[4,256]{1,0:T(4,128)(2,1)S(1)}, bf16[4,256]{1,0:T(4,128)(2,1)}, u32[]{:S(2)}) copy-start(bf16[4,256]{1,0:T(4,128)(2,1)} %nk_ref.1) | copy-start | bytes 6148
  36.4 16.2 %copy-start.7 = (bf16[4,256]{1,0:T(4,128)(2,1)S(1)}, bf16[4,256]{1,0:T(4,128)(2,1)}, u32[]{:S(2)}) copy-start(bf16[4,256]{1,0:T(4,128)(2,1)} %nv_ref.1) | copy-start | bytes 6148
  36.4 16.2 %copy-start.11 = (s32[4]{0:T(128)S(1)}, s32[4]{0:T(128)}, u32[]{:S(2)}) copy-start(s32[4]{0:T(128)} %lengths_ref.1) | copy-start | bytes 52
  36.4 23.6 %copy-start.5 = (s32[6,3]{0,1:T(4,128)S(1)}, s32[6,3]{0,1:T(4,128)}, u32[]{:S(2)}) copy-start(s32[6,3]{0,1:T(4,128)} %param.14) | copy-start | bytes 220
  36.4 23.6 %copy-start.8 = (f32[6,3]{0,1:T(4,128)S(1)}, f32[6,3]{0,1:T(4,128)}, u32[]{:S(2)}) copy-start(f32[6,3]{0,1:T(4,128)} %param.15) | copy-start | bytes 220
  36.4 23.6 %copy-start.10 = (s32[4]{0:T(128)S(1)}, s32[4]{0:T(128)}, u32[]{:S(2)}) copy-start(s32[4]{0:T(128)} %owners_ref.3) | copy-start | bytes 52
  36.4 1.5 %collective-permute-start.4 = (f32[16,2560]{1,0:T(8,128)S(1)}, f32[16,2560]{1,0:T(8,128)S(1)}, u32[]{:S(2)}, u32[]{:S(2)}) collective-permute-start(f32[16,2560]{1,0:T(8,128)S(1)} %get-tuple-element.12.ga), channel_id=1, source_target_pairs={{0,1},{1,0},{2,3},{3,2},{4,5},{5,4},{6,7},{7,6},{8,9},{9,8},{10,11... | collective-permute-start | bytes 491528 | tf_op jit(solution)/shard_map/ppermute | solution.py:251
  36.5 1.6 %collective-permute-start.5 = (f32[16,2560]{1,0:T(8,128)S(1)}, f32[16,2560]{1,0:T(8,128)S(1)}, u32[]{:S(2)}, u32[]{:S(2)}) collective-permute-start(f32[16,2560]{1,0:T(8,128)S(1)} %get-tuple-element.13.ua), channel_id=1, source_target_pairs={{0,1},{1,0},{2,3},{3,2},{4,5},{5,4},{6,7},{7,6},{8,9},{9,8},{10,11... | collective-permute-start | bytes 491528 | tf_op jit(solution)/shard_map/ppermute | solution.py:251
  49.2 10.8 %all-to-all-start = ((bf16[8,2,3584]{2,1,0:T(2,128)(2,1)}), bf16[8,2,3584]{2,1,0:T(2,128)(2,1)S(1)}, u32[]{:S(2)}, u32[]{:S(2)}) async-start(bf16[8,2,3584]{2,1,0:T(2,128)(2,1)} %down.1), calls=%async_computation | async-start | bytes 229376 | tf_op jit(solution)/shard_map/all_to_all | solution.py:289

commit v2 on v1

--- a/solution.py
+++ b/solution.py
@@ -15,10 +15,12 @@
 
 VMEM = pl.BlockSpec(memory_space=pltpu.VMEM)
 SMEM = pl.BlockSpec(memory_space=pltpu.SMEM)
-
-
-def params(mib):
-    return pltpu.CompilerParams(vmem_limit_bytes=mib * 1024 * 1024)
+HBM = pl.BlockSpec(memory_space=pltpu.HBM)
+
+
+def params(mib, rows=16):
+    scaled = min(48, mib * max(1, rows // 16))
+    return pltpu.CompilerParams(vmem_limit_bytes=scaled * 1024 * 1024)
 
 
 def expert_of(owners_ref, block):
@@ -35,7 +37,23 @@
     return ids
 
 
-def pick_kernel(group_size, owners_ref, routes_ref, act_ref, out_ref):
+def fetch(pairs, sems):
+    copies = [pltpu.make_async_copy(*pair, sems.at[n]) for n, pair in enumerate(pairs)]
+    for copy in copies:
+        copy.start()
+    return copies
+
+
+def in_hbm(*arrays):
+    return [pltpu.with_memory_space_constraint(x, pltpu.HBM) for x in arrays]
+
+
+def pick_kernel(group_size, owners_hbm, routes_hbm, act_hbm, out_ref, owners_ref, routes_ref, act_ref, sems):
+    copies = fetch(
+        ((owners_hbm, owners_ref), (routes_hbm, routes_ref), (act_hbm, act_ref)), sems
+    )
+    for copy in copies:
+        copy.wait()
     tokens = act_ref.shape[0]
     here = lax.axis_index("wide") // group_size
     rows = lax.broadcasted_iota(jnp.int32, (SLOTS, tokens), 0)
@@ -55,11 +73,20 @@
     return pl.pallas_call(
         functools.partial(pick_kernel, group_size),
         out_shape=jax.ShapeDtypeStruct((SLOTS, act_rows.shape[1]), BF16),
-        in_specs=[SMEM, VMEM, VMEM],
+        in_specs=[HBM] * 3,
         out_specs=VMEM,
-        compiler_params=params(4),
+        scratch_shapes=[
+            pltpu.SMEM(owners.shape, owners.dtype),
+            pltpu.VMEM(routes_t.shape, routes_t.dtype),
+            pltpu.VMEM(act_rows.shape, act_rows.dtype),
+            pltpu.SemaphoreType.DMA((3,)),
+        ],
+        compiler_params=params(2),
+        cost_estimate=pl.CostEstimate(
+            flops=40_000_000_000, bytes_accessed=120_000_000, transcendentals=0
+        ),
         name="pick_rows",
-    )(owners, routes_t, act_rows)
+    )(*in_hbm(owners, routes_t, act_rows))
 
 
 def message_kernel(near_ref, far_ref, *out_refs):
@@ -77,93 +104,86 @@
         out_shape=(shape,) * EXPERTS,
         in_specs=[VMEM, VMEM],
         out_specs=(VMEM,) * EXPERTS,
-        compiler_params=params(16),
+        compiler_params=params(2, EXPERTS * rows),
         name="messages",
     )(near, far)
 
 
-def gate_up_kernel(depth, *refs):
+def gate_up_kernel(*refs):
     msg_refs = refs[:EXPERTS]
-    gate_ref, up_ref, gate_out, up_out, rows_ref = refs[EXPERTS:]
-    step = pl.program_id(0)
-
-    @pl.when(step == 0)
-    def _():
-        rows = jnp.concatenate([ref[...].astype(F32) for ref in msg_refs], axis=0).astype(BF16)
-        for k in range(rows_ref.shape[0]):
-            rows_ref[k] = rows[:, k * depth : (k + 1) * depth]
-        gate_out[...] = jnp.zeros_like(gate_out)
-        up_out[...] = jnp.zeros_like(up_out)
-
-    rows = rows_ref[step]
-    gate_out[...] += jnp.dot(rows, gate_ref[...], preferred_element_type=F32)
-    up_out[...] += jnp.dot(rows, up_ref[...], preferred_element_type=F32)
-
-
-def gate_up(msgs, w_gate, w_up, depth=256):
-    features, hidden = w_gate.shape
+    gate_ref, up_ref, down_hbm, gate_out, up_out, down_out, sem = refs[EXPERTS:]
+    copy = pltpu.make_async_copy(down_hbm.at[pl.ds(0, down_out.shape[0])], down_out, sem)
+    copy.start()
+    rows = jnp.concatenate([ref[...].astype(F32) for ref in msg_refs], axis=0).astype(BF16)
+    gate_out[...] = jnp.dot(rows, gate_ref[...], preferred_element_type=F32)
+    up_out[...] = jnp.dot(rows, up_ref[...], preferred_element_type=F32)
+    copy.wait()
+
+
+def gate_up(msgs, w_gate, w_up, w_down, early):
     rows = sum(m.shape[0] for m in msgs)
-    shape = jax.ShapeDtypeStruct((rows, hidden), F32)
-    whole = [pl.BlockSpec(m.shape, lambda k: (0, 0)) for m in msgs]
-    weight = pl.BlockSpec((depth, hidden), lambda k: (k, 0))
-    out = pl.BlockSpec((rows, hidden), lambda k: (0, 0))
-    return pl.pallas_call(
-        functools.partial(gate_up_kernel, depth),
-        out_shape=(shape, shape),
-        grid=(features // depth,),
-        in_specs=whole + [weight, weight],
-        out_specs=(out, out),
-        scratch_shapes=[pltpu.VMEM((features // depth, rows, depth), BF16)],
-        compiler_params=params(40),
+    shape = jax.ShapeDtypeStruct((rows, w_gate.shape[1]), F32)
+    return pl.pallas_call(
+        gate_up_kernel,
+        out_shape=(shape, shape, pltpu.VMEM((early, w_down.shape[1]), BF16)),
+        in_specs=[VMEM] * (EXPERTS + 2) + [HBM],
+        out_specs=(VMEM,) * 3,
+        scratch_shapes=[pltpu.SemaphoreType.DMA],
+        compiler_params=params(4, rows),
         name="gate_up",
-    )(*msgs, w_gate, w_up)
-
-
-def down_kernel(group_size, depth, ga, gb, ua, ub, down_ref, out_ref, hid_ref, acc_ref):
-    step = pl.program_id(0)
-    steps = hid_ref.shape[0]
-
-    @pl.when(step == 0)
-    def _():
-        gate = ga[...] + gb[...]
-        up = ua[...] + ub[...]
-        hidden = (gate / (1.0 + jnp.exp(-gate)) * up).astype(BF16)
-        for k in range(steps):
-            hid_ref[k] = hidden[:, k * depth : (k + 1) * depth]
-        acc_ref[...] = jnp.zeros_like(acc_ref)
-
-    acc_ref[...] += jnp.dot(hid_ref[step], down_ref[...], preferred_element_type=F32)
-
-    @pl.when(step == steps - 1)
-    def _():
-        wide = lax.axis_index("wide")
-        block, place = wide // group_size, wide % group_size
-        acc = acc_ref[...]
-        for m in range(EXPERTS):
-            for j in range(group_size):
-                target = (block ^ m) * group_size + (place ^ j)
-                start = (m * group_size + j) * CAP
-                out_ref[target] = acc[start : start + CAP].astype(BF16)
-
-
-def down(gate_pair, up_pair, w_down, group_size, depth):
+    )(*msgs, w_gate, w_up, *in_hbm(w_down))
+
+
+def down_kernel(group_size, ga, gb, ua, ub, early_ref, down_hbm, out_ref, late_ref, acc_ref, sem):
+    early, late = early_ref.shape[0], late_ref.shape[0]
+    copy = pltpu.make_async_copy(down_hbm.at[pl.ds(early, late)], late_ref, sem)
+    copy.start()
+    gate = ga[...] + gb[...]
+    up = ua[...] + ub[...]
+    hidden = (gate / (1.0 + jnp.exp(-gate)) * up).astype(BF16)
+    features = acc_ref.shape[1]
+    step = next(n for n in (512, 256, 128, features) if features % n == 0)
+    for n in range(0, features, step):
+        acc_ref[:, n : n + step] = jnp.dot(
+            hidden[:, :early], early_ref[:, n : n + step], preferred_element_type=F32
+        )
+    copy.wait()
+    for n in range(0, features, step):
+        acc_ref[:, n : n + step] += jnp.dot(
+            hidden[:, early:], late_ref[:, n : n + step], preferred_element_type=F32
+        )
+    acc = acc_ref[...]
+    wide = lax.axis_index("wide")
+    block, place = wide // group_size, wide % group_size
+    for m in range(EXPERTS):
+        for j in range(group_size):
+            target = (block ^ m) * group_size + (place ^ j)
+            start = (m * group_size + j) * CAP
+            out_ref[target] = acc[start : start + CAP].astype(BF16)
+
+
+def down(gate_pair, up_pair, w_early, w_down, group_size):
+    rows = gate_pair[0].shape[0]
     hidden, features = w_down.shape
-    rows = gate_pair[0].shape[0]
-    devices = rows // CAP
-    whole = pl.BlockSpec((rows, hidden), lambda k: (0, 0))
-    return pl.pallas_call(
-        functools.partial(down_kernel, group_size, depth),
-        out_shape=jax.ShapeDtypeStruct((devices, CAP, features), BF16),
-        grid=(hidden // depth,),
-        in_specs=[whole] * 4 + [pl.BlockSpec((depth, features), lambda k: (k, 0))],
-        out_specs=pl.BlockSpec((devices, CAP, features), lambda k: (0, 0, 0)),
+    late = hidden - w_early.shape[0]
+    return pl.pallas_call(
+        functools.partial(down_kernel, group_size),
+        out_shape=jax.ShapeDtypeStruct((rows // CAP, CAP, features), BF16),
+        in_specs=[VMEM] * 5 + [HBM],
+        out_specs=VMEM,
         scratch_shapes=[
-            pltpu.VMEM((hidden // depth, rows, depth), BF16),
+            pltpu.VMEM((late, features), BF16),
             pltpu.VMEM((rows, features), F32),
+            pltpu.SemaphoreType.DMA,
         ],
-        compiler_params=params(40),
+        compiler_params=params(8, rows),
         name="down",
-    )(*gate_pair, *up_pair, w_down)
+    )(
+        *gate_pair,
+        *up_pair,
+        pltpu.with_memory_space_constraint(w_early, pltpu.VMEM),
+        *in_hbm(w_down),
+    )
 
 
 def combine_kernel(group_size, owners_ref, routes_ref, weights_ref, back_ref, out_ref, rows_ref):
@@ -204,12 +224,17 @@
         in_specs=[SMEM, VMEM, VMEM, VMEM],
         out_specs=VMEM,
         scratch_shapes=[pltpu.VMEM((devices * CAP, features), F32)],
-        compiler_params=params(16),
+        compiler_params=params(2, devices * CAP),
         name="combine",
     )(owners, routes_t, weights_t, back)
 
 
-def attend_kernel(lengths_ref, q_ref, nk_ref, nv_ref, keys_ref, values_ref, out_ref, turn_ref):
+def attend_kernel(*refs):
+    hbm, out_ref, scratch, turn_ref, sems = refs[:6], refs[6], refs[7:13], refs[13], refs[14]
+    lengths_ref, q_ref, nk_ref, nv_ref, keys_ref, values_ref = scratch
+    copies = fetch(tuple(zip(hbm, scratch)), sems)
+    for copy in copies:
+        copy.wait()
     requests, heads, size = q_ref.shape
     scaling = size ** (-0.5)
     for r in range(requests):
@@ -236,15 +261,18 @@
 
 def attend(queries, new_keys, new_values, key_cache, value_cache, lengths):
     requests, heads, size = queries.shape
+    operands = (queries, new_keys, new_values, key_cache, value_cache)
     return pl.pallas_call(
         attend_kernel,
         out_shape=jax.ShapeDtypeStruct((requests, heads * size), BF16),
-        in_specs=[SMEM] + [VMEM] * 5,
+        in_specs=[HBM] * 6,
         out_specs=VMEM,
-        scratch_shapes=[pltpu.VMEM((heads, requests, size), F32)],
-        compiler_params=params(8),
+        scratch_shapes=[pltpu.SMEM(lengths.shape, lengths.dtype)]
+        + [pltpu.VMEM(x.shape, x.dtype) for x in operands]
+        + [pltpu.VMEM((heads, requests, size), F32), pltpu.SemaphoreType.DMA((6,))],
+        compiler_params=params(2),
         name="attend",
-    )(lengths, queries, new_keys, new_values, key_cache, value_cache)
+    )(*in_hbm(lengths, *operands))
 
 
 def swap(x, axis, devices, mask):
@@ -269,6 +297,7 @@
     devices = lax.axis_size("wide")
     group_size = devices // EXPERTS
     routes_t, weights_t = routes.T, route_weights.T
+    w_gate, w_up = (pltpu.with_memory_space_constraint(w, pltpu.VMEM) for w in (w_gate, w_up))
     near = pick_rows(owners, routes_t, act_rows, group_size)[None]
     mask = 1
     while 2 * mask < group_size:
@@ -279,13 +308,12 @@
     for m in range(1, EXPERTS):
         msgs[m] = swap(msgs[m], "wide", devices, m * group_size)
     context = attend(queries, new_keys, new_values, key_cache, value_cache, lengths)
-    gate, up = gate_up(msgs, w_gate, w_up)
+    msgs, context = lax.optimization_barrier((msgs, context))
+    early = w_down.shape[0] * 3 // 4 // 16 * 16
+    gate, up, w_early = gate_up(msgs, w_gate, w_up, w_down, early)
     gate_pair = (gate, swap(gate, "narrow", 2, 1))
     up_pair = (up, swap(up, "narrow", 2, 1))
-    depth = min(256, w_down.shape[0])
-    if w_down.shape[0] % depth:
-        depth = w_down.shape[0]
-    partial_value = down(gate_pair, up_pair, w_down, group_size, depth)
+    partial_value = down(gate_pair, up_pair, w_early, w_down, group_size)
     back = lax.all_to_all(partial_value, "wide", split_axis=0, concat_axis=0, tiled=True)
     ffn_out = combine(owners, routes_t, weights_t, back, group_size)
     return (ffn_out, context)

time: 61.9 us -> 40.8 us (0.66)
  Pallas kernels: 33.3 us -> 14.7 us
  blocking collectives: 0 us -> 11.5 us
  waiting for transfers between devices: 13.4 us -> 5.31 us
  starting transfers between devices: 11.7 us -> 8.33 us
  local copies, waits for them, and re-layouts: 2.21 us -> 0.03 us
    pallas_call x2, Pallas kernels: 28.2 us -> 8.31 us  [the longest x1 5.27 us: gate_up(): pl.pallas_call(gate_up_kernel, out_shape=(shape, shape, pltpu.VMEM((early...]
    all_to_all x0 -> x1, blocking collectives: none -> 11.5 us  [per_device(): lax.all_to_all(partial_value, 'wide', split_axis=0, concat_axis=0, tiled=...]
    all_to_all x1 -> x0, waiting for transfers between devices: 4.51 us -> none  [per_device(): lax.all_to_all(partial_value, 'wide', split_axis=0, concat_axis=0, tiled=...]
    ppermute x6, waiting for transfers between devices: 8.94 us -> 5.31 us  [swap(): return lax.ppermute(x, axis, [(i, i ^ mask) for i in range(devices)])]
    all_to_all x1 -> x0, starting transfers between devices: 3.37 us -> none  [per_device(): lax.all_to_all(partial_value, 'wide', split_axis=0, concat_axis=0, tiled=...]
    unnamed x24 -> x10, local copies, waits for them, and re-layouts: 2.21 us -> 0.03 us
    pallas_call x1, Pallas kernels: 2.83 us -> 3.61 us  [attend(): pl.pallas_call(attend_kernel, out_shape=jax.ShapeDtypeStruct((requests, h...]
  transfers between devices with their start and end apart: 7 -> 6, of which waited for: 6 -> 4; matrix products, arithmetic and copies ran while one was open for 0% -> 0% of each run, Pallas kernels for 5% -> 9%
where the time goes in v2:
time: 40.8 us; the launch traced here: 40.5 us
  Pallas kernels  14.7 us (36%)
  blocking collectives  11.5 us (28%)
  starting transfers between devices  8.33 us (20%)
  waiting for transfers between devices  5.31 us (13%)
  between operations  0.74 us (2%)
    all_to_all x1, blocking collectives, per_device(): lax.all_to_all(partial_value, 'wide', split_axis=0, concat_axis=0, tiled=...  11.5 us
    ppermute x6, starting transfers between devices, swap(): return lax.ppermute(x, axis, [(i, i ^ mask) for i in range(devices)])  8.33 us
    ppermute x6, waiting for transfers between devices, swap(): return lax.ppermute(x, axis, [(i, i ^ mask) for i in range(devices)])  5.31 us
    pallas_call x1, Pallas kernels, gate_up(): pl.pallas_call(gate_up_kernel, out_shape=(shape, shape, pltpu.VMEM((early...  5.27 us
    pallas_call x1, Pallas kernels, attend(): pl.pallas_call(attend_kernel, out_shape=jax.ShapeDtypeStruct((requests, h...  3.61 us
    pallas_call x1, Pallas kernels, down(): pl.pallas_call(functools.partial(down_kernel, group_size), out_shape=jax....  3.04 us
    pallas_call x1, Pallas kernels, combine(): pl.pallas_call(functools.partial(combine_kernel, group_size), out_shape=j...  1.42 us
    pallas_call x1, Pallas kernels, pick_rows(): pl.pallas_call(functools.partial(pick_kernel, group_size), out_shape=jax....  1.26 us
  transfers between devices with their start and end apart: 6, of which 4 were waited for; matrix products, arithmetic and copies ran while one was open for 0% of the time, Pallas kernels for 9%

profile of v2, /device:TPU:0, one launch (start us, length us, event | category | flops | bytes accessed | tf_op | source)
XLA Modules:
  0.0 40.5 jit_solution(8323391619016102645)
XLA Ops:
  0.6 1.3 %pick_rows.1 = bf16[8,3584]{1,0:T(8,128)(2,1)S(1)} custom-call(s32[4]{0:T(128)} %owners_ref.1, s32[3,6]{1,0:T(4,128)} %bitcast.5, bf16[6,3584]{1,0:T(8,128)(2,1)} %act_hbm.1), custom_call_target="tpu_custom_call" | custom-call | flops 40000000000 | bytes 120000000 | tf_op jit(solution)/shard_map/pick_rows/pallas_call | solution.py:73
  1.9 3.0 %collective-permute-start = (bf16[1,8,3584]{2,1,0:T(8,128)(2,1)S(1)}, bf16[1,8,3584]{2,1,0:T(8,128)(2,1)S(1)}, u32[]{:S(2)}, u32[]{:S(2)}) collective-permute-start(bf16[1,8,3584]{2,1,0:T(8,128)(2,1)S(1)} %bitcast.3), channel_id=1, source_target_pairs={{0,2},{2,0},{4,6},{6,4},{8,10},{10,8},{12,14},{14,12},{1,3},{3,1},... | collective-permute-start | bytes 172040 | tf_op jit(solution)/shard_map/ppermute | solution.py:279
  4.9 2.2 %collective-permute-done.far_ref = bf16[1,8,3584]{2,1,0:T(8,128)(2,1)S(1)} collective-permute-done((bf16[1,8,3584]{2,1,0:T(8,128)(2,1)S(1)}, bf16[1,8,3584]{2,1,0:T(8,128)(2,1)S(1)}, u32[]{:S(2)}, u32[]{:S(2)}) %collective-permute-start) | collective-permute-done | bytes 57376 | tf_op jit(solution)/shard_map/ppermute | solution.py:279
  7.1 0.1 messages.1
  7.1 2.2 %collective-permute-start.1 = (bf16[4,3584]{1,0:T(4,128)(2,1)S(1)}, bf16[4,3584]{1,0:T(4,128)(2,1)S(1)}, u32[]{:S(2)}, u32[]{:S(2)}) collective-permute-start(bf16[4,3584]{1,0:T(4,128)(2,1)S(1)} %get-tuple-element.15), channel_id=1, source_target_pairs={{0,4},{2,6},{4,0},{6,2},{8,12},{10,14},{12,8},{14,10},{1,5},{3,7},... | collective-permute-start | bytes 86024 | tf_op jit(solution)/shard_map/ppermute | solution.py:279
  9.3 2.6 %collective-permute-start.2 = (bf16[4,3584]{1,0:T(4,128)(2,1)S(1)}, bf16[4,3584]{1,0:T(4,128)(2,1)S(1)}, u32[]{:S(2)}, u32[]{:S(2)}) collective-permute-start(bf16[4,3584]{1,0:T(4,128)(2,1)S(1)} %get-tuple-element.16), channel_id=1, source_target_pairs={{0,8},{2,10},{4,12},{6,14},{8,0},{10,2},{12,4},{14,6},{1,9},{3,11}... | collective-permute-start | bytes 86024 | tf_op jit(solution)/shard_map/ppermute | solution.py:279
  11.9 0.0 collective-permute-start.3
  11.9 3.6 %attend.1 = bf16[4,8192]{1,0:T(4,128)(2,1)} custom-call(s32[4]{0:T(128)} %refs_0_.1, bf16[4,32,256]{2,1,0:T(8,128)(2,1)} %refs_1_.1, bf16[4,256]{1,0:T(4,128)(2,1)} %refs_2_.1, bf16[4,256]{1,0:T(4,128)(2,1)} %refs_3_.1, bf16[4,256,256]{2,1,0:T(8,128)(2,1)} %refs_4_.2, bf16[4,256,256]{2,1,0:T(8,128)(2,1)} %refs_5_.2), custom_call_target="tpu_custom_call" | custom-call | tf_op jit(solution)/shard_map/attend/pallas_call | solution.py:265
  15.5 0.0 collective-permute-done.1.refs_1_
  15.5 0.0 collective-permute-done.2.refs_2_
  15.6 2.0 %collective-permute-done.3.refs_3_ = bf16[4,3584]{1,0:T(4,128)(2,1)S(1)} collective-permute-done((bf16[4,3584]{1,0:T(4,128)(2,1)S(1)}, bf16[4,3584]{1,0:T(4,128)(2,1)S(1)}, u32[]{:S(2)}, u32[]{:S(2)}) %collective-permute-start.3) | collective-permute-done | bytes 28704 | tf_op jit(solution)/shard_map/ppermute | solution.py:279
  17.6 0.0 copy-done
  17.6 5.3 %gate_up.1 = (f32[16,2560]{1,0:T(8,128)S(1)}, f32[16,2560]{1,0:T(8,128)S(1)}, bf16[1920,3584]{1,0:T(8,128)(2,1)S(1)}) custom-call(bf16[4,3584]{1,0:T(4,128)(2,1)S(1)} %get-tuple-element.18.refs_0_, bf16[4,3584]{1,0:T(4,128)(2,1)S(1)} %collective-permute-done.1.refs_1_, bf16[4,3584]{1,0:T(4,128)(2,1)S(1)} %collective-permute-done.2.refs_2_, ...), custom_call_target="tpu_custom_call" | custom-call | tf_op jit(solution)/shard_map/gate_up/pallas_call | solution.py:126
  22.9 0.0 copy-start.2
  22.9 0.0 copy-start.3
  22.9 0.0 copy-start.4
  22.9 0.1 collective-permute-start.4
  23.0 0.5 %collective-permute-start.5 = (f32[16,2560]{1,0:T(8,128)S(1)}, f32[16,2560]{1,0:T(8,128)S(1)}, u32[]{:S(2)}, u32[]{:S(2)}) collective-permute-start(f32[16,2560]{1,0:T(8,128)S(1)} %get-tuple-element.23.ua), channel_id=1, source_target_pairs={{0,1},{1,0},{2,3},{3,2},{4,5},{5,4},{6,7},{7,6},{8,9},{9,8},{10,11... | collective-permute-start | bytes 491528 | tf_op jit(solution)/shard_map/ppermute | solution.py:279
  23.5 0.9 %collective-permute-done.4.gb = f32[16,2560]{1,0:T(8,128)S(1)} collective-permute-done((f32[16,2560]{1,0:T(8,128)S(1)}, f32[16,2560]{1,0:T(8,128)S(1)}, u32[]{:S(2)}, u32[]{:S(2)}) %collective-permute-start.4) | collective-permute-done | bytes 163872 | tf_op jit(solution)/shard_map/ppermute | solution.py:279
  24.4 0.2 collective-permute-done.5.ub
  24.6 3.0 %down.1 = bf16[8,2,3584]{2,1,0:T(2,128)(2,1)S(1)} custom-call(f32[16,2560]{1,0:T(8,128)S(1)} %get-tuple-element.22.ga, f32[16,2560]{1,0:T(8,128)S(1)} %collective-permute-done.4.gb, f32[16,2560]{1,0:T(8,128)S(1)} %get-tuple-element.23.ua, f32[16,2560]{1,0:T(8,128)S(1)} %collective-permute-done.5.ub, bf16[1920,3584]{1,0:T(8,128)(2,1)S(1)} %get-tuple-element.24.early_ref, ...), custom_call_target="tpu_custom_call" | custom-call | tf_op jit(solution)/shard_map/down/pallas_call | solution.py:169
  27.6 11.5 %all_to_all.5.back_ref = bf16[8,2,3584]{2,1,0:T(2,128)(2,1)S(1)} all-to-all(bf16[8,2,3584]{2,1,0:T(2,128)(2,1)S(1)} %down.1), channel_id=1, replica_groups=mesh['groups'=2,'wide'=8,'narrow'=2] {'wide'}, dimensions={0} | all-to-all | bytes 229376 | tf_op jit(solution)/shard_map/all_to_all | solution.py:317
  39.1 0.0 copy-done.4
  39.1 1.4 %combine.1 = bf16[6,3584]{1,0:T(8,128)(2,1)} custom-call(s32[4]{0:T(128)S(1)} %copy-done.4, s32[3,6]{1,0:T(4,128)S(1)} %bitcast.6, f32[3,6]{1,0:T(4,128)S(1)} %bitcast.7, bf16[8,2,3584]{2,1,0:T(2,128)(2,1)S(1)} %all_to_all.5.back_ref), custom_call_target="tpu_custom_call" | custom-call | tf_op jit(solution)/shard_map/combine/pallas_call | solution.py:221
  (5 shorter events, 0.0 us)
Async XLA Ops:
  0.6 17.0 %copy-start = (bf16[3584,2560]{1,0:T(8,128)(2,1)S(1)}, bf16[3584,2560]{1,0:T(8,128)(2,1)}, u32[]{:S(2)}) copy-start(bf16[3584,2560]{1,0:T(8,128)(2,1)} %refs_4_.3) | copy-start | bytes 55050244
  0.6 16.9 %copy-start.1 = (bf16[3584,2560]{1,0:T(8,128)(2,1)S(1)}, bf16[3584,2560]{1,0:T(8,128)(2,1)}, u32[]{:S(2)}) copy-start(bf16[3584,2560]{1,0:T(8,128)(2,1)} %refs_5_.3) | copy-start | bytes 55050244
  1.9 5.2 %collective-permute-start = (bf16[1,8,3584]{2,1,0:T(8,128)(2,1)S(1)}, bf16[1,8,3584]{2,1,0:T(8,128)(2,1)S(1)}, u32[]{:S(2)}, u32[]{:S(2)}) collective-permute-start(bf16[1,8,3584]{2,1,0:T(8,128)(2,1)S(1)} %bitcast.3), channel_id=1, source_target_pairs={{0,2},{2,0},{4,6},{6,4},{8,10},{10,8},{12,14},{14,12},{1,3},{3,1},... | collective-permute-start | bytes 172040 | tf_op jit(solution)/shard_map/ppermute | solution.py:279
  7.1 8.4 %collective-permute-start.1 = (bf16[4,3584]{1,0:T(4,128)(2,1)S(1)}, bf16[4,3584]{1,0:T(4,128)(2,1)S(1)}, u32[]{:S(2)}, u32[]{:S(2)}) collective-permute-start(bf16[4,3584]{1,0:T(4,128)(2,1)S(1)} %get-tuple-element.15), channel_id=1, source_target_pairs={{0,4},{2,6},{4,0},{6,2},{8,12},{10,14},{12,8},{14,10},{1,5},{3,7},... | collective-permute-start | bytes 86024 | tf_op jit(solution)/shard_map/ppermute | solution.py:279
  9.3 6.2 %collective-permute-start.2 = (bf16[4,3584]{1,0:T(4,128)(2,1)S(1)}, bf16[4,3584]{1,0:T(4,128)(2,1)S(1)}, u32[]{:S(2)}, u32[]{:S(2)}) collective-permute-start(bf16[4,3584]{1,0:T(4,128)(2,1)S(1)} %get-tuple-element.16), channel_id=1, source_target_pairs={{0,8},{2,10},{4,12},{6,14},{8,0},{10,2},{12,4},{14,6},{1,9},{3,11}... | collective-permute-start | bytes 86024 | tf_op jit(solution)/shard_map/ppermute | solution.py:279
  11.9 5.7 %collective-permute-start.3 = (bf16[4,3584]{1,0:T(4,128)(2,1)S(1)}, bf16[4,3584]{1,0:T(4,128)(2,1)S(1)}, u32[]{:S(2)}, u32[]{:S(2)}) collective-permute-start(bf16[4,3584]{1,0:T(4,128)(2,1)S(1)} %get-tuple-element.17), channel_id=1, source_target_pairs={{0,12},{2,14},{4,8},{6,10},{8,4},{10,6},{12,0},{14,2},{1,13},{3,15... | collective-permute-start | bytes 86024 | tf_op jit(solution)/shard_map/ppermute | solution.py:279
  22.9 16.3 %copy-start.2 = (s32[6,3]{0,1:T(4,128)S(1)}, s32[6,3]{0,1:T(4,128)}, u32[]{:S(2)}) copy-start(s32[6,3]{0,1:T(4,128)} %param.14) | copy-start | bytes 220
  22.9 16.2 %copy-start.3 = (f32[6,3]{0,1:T(4,128)S(1)}, f32[6,3]{0,1:T(4,128)}, u32[]{:S(2)}) copy-start(f32[6,3]{0,1:T(4,128)} %param.15) | copy-start | bytes 220
  22.9 16.2 %copy-start.4 = (s32[4]{0:T(128)S(1)}, s32[4]{0:T(128)}, u32[]{:S(2)}) copy-start(s32[4]{0:T(128)} %owners_ref.1) | copy-start | bytes 52
  22.9 1.5 %collective-permute-start.4 = (f32[16,2560]{1,0:T(8,128)S(1)}, f32[16,2560]{1,0:T(8,128)S(1)}, u32[]{:S(2)}, u32[]{:S(2)}) collective-permute-start(f32[16,2560]{1,0:T(8,128)S(1)} %get-tuple-element.22.ga), channel_id=1, source_target_pairs={{0,1},{1,0},{2,3},{3,2},{4,5},{5,4},{6,7},{7,6},{8,9},{9,8},{10,11... | collective-permute-start | bytes 491528 | tf_op jit(solution)/shard_map/ppermute | solution.py:279
  23.0 1.6 %collective-permute-start.5 = (f32[16,2560]{1,0:T(8,128)S(1)}, f32[16,2560]{1,0:T(8,128)S(1)}, u32[]{:S(2)}, u32[]{:S(2)}) collective-permute-start(f32[16,2560]{1,0:T(8,128)S(1)} %get-tuple-element.23.ua), channel_id=1, source_target_pairs={{0,1},{1,0},{2,3},{3,2},{4,5},{5,4},{6,7},{7,6},{8,9},{9,8},{10,11... | collective-permute-start | bytes 491528 | tf_op jit(solution)/shard_map/ppermute | solution.py:279

commit v3 on v0

v3 whole, which is shorter than its diff:
```python
import functools

import jax
import jax.numpy as jnp
from jax import lax
from jax.experimental import pallas as pl
from jax.experimental.pallas import tpu as pltpu
from jax.sharding import PartitionSpec as P

EXPERTS = 4
CAP = 2
SLOTS = EXPERTS * CAP
F32 = jnp.float32
BF16 = jnp.bfloat16

VMEM = pl.BlockSpec(memory_space=pltpu.VMEM)
HBM = pl.BlockSpec(memory_space=pltpu.HBM)


def params(mib, rows=16):
    scaled = min(48, mib * max(1, rows // 16))
    return pltpu.CompilerParams(vmem_limit_bytes=scaled * 1024 * 1024)


def experts_of(owners_ref, blocks):
    ids = jnp.zeros_like(blocks)
    for expert in range(EXPERTS):
        ids = jnp.where(owners_ref[:, expert : expert + 1] == blocks, expert, ids)
    return ids


def fetch(pairs, sems):
    copies = [pltpu.make_async_copy(*pair, sems.at[n]) for n, pair in enumerate(pairs)]
    for copy in copies:
        copy.start()
    return copies


def in_hbm(*arrays):
    return [pltpu.with_memory_space_constraint(x, pltpu.HBM) for x in arrays]


def in_vmem(*arrays):
    return [pltpu.with_memory_space_constraint(x, pltpu.VMEM) for x in arrays]


def pick_kernel(
    group_size, owners_hbm, routes_hbm, act_hbm, out_ref, owners_ref, routes_ref, act_ref, sems
):
    copies = fetch(
        ((owners_hbm, owners_ref), (routes_hbm, routes_ref), (act_hbm, act_ref)), sems
    )
    for copy in copies:
        copy.wait()
    tokens = act_ref.shape[0]
    rows = lax.broadcasted_iota(jnp.int32, (SLOTS, tokens), 0)
    cols = lax.broadcasted_iota(jnp.int32, (SLOTS, tokens), 1)
    ids = experts_of(owners_ref, rows // CAP)
    hit = jnp.zeros((SLOTS, tokens), F32)
    for k in range(routes_ref.shape[0]):
        hit = jnp.where(routes_ref[k : k + 1, :] == ids, 1.0, hit)
    rank = jnp.zeros((SLOTS, tokens), F32)
    for t in range(tokens - 1):
        rank += jnp.where(cols > t, hit[:, t : t + 1], 0.0)
    picks = jnp.where(rank == (rows % CAP).astype(F32), hit, 0.0).astype(BF16)
    chosen = jnp.dot(picks, act_ref[...], preferred_element_type=F32)
    for m in range(EXPERTS):
        for j in range(group_size):
            out_ref[m * group_size + j] = chosen[m * CAP : (m + 1) * CAP].astype(BF16)


def pick_rows(owners, routes_t, act_rows, group_size):
    return pl.pallas_call(
        functools.partial(pick_kernel, group_size),
        out_shape=jax.ShapeDtypeStruct((EXPERTS * group_size, CAP, act_rows.shape[1]), BF16),
        in_specs=[HBM] * 3,
        out_specs=VMEM,
        scratch_shapes=[
            pltpu.VMEM(owners.shape, owners.dtype),
            pltpu.VMEM(routes_t.shape, routes_t.dtype),
            pltpu.VMEM(act_rows.shape, act_rows.dtype),
            pltpu.SemaphoreType.DMA((3,)),
        ],
        compiler_params=params(2),
        cost_estimate=pl.CostEstimate(
            flops=100000000000, bytes_accessed=120_000_000, transcendentals=0
        ),
        name="pick_rows",
    )(*in_hbm(owners, routes_t, act_rows))


def attention_steps(lengths_ref, q_ref, nk_ref, nv_ref, keys_ref, values_ref, out_ref, turn_ref):
    requests, heads, size = q_ref.shape
    scaling = size ** (-0.5)
    span = range(requests)
    scores = [
        lax.dot_general(
            q_ref[r], keys_ref[r], (((1,), (1,)), ((), ())), preferred_element_type=F32
        )
        for r in span
    ]
    yield
    place = lax.broadcasted_iota(jnp.int32, scores[0].shape, 1)
    scores = [
        jnp.where(place < lengths_ref[:, r : r + 1], scores[r] * scaling, -jnp.inf) for r in span
    ]
    owns = [
        jnp.sum(q_ref[r].astype(F32) * nk_ref[r : r + 1, :].astype(F32), axis=1, keepdims=True)
        for r in span
    ]
    score = jnp.concatenate(scores, axis=0)
    own = jnp.concatenate(owns, axis=0) * scaling
    top = jnp.maximum(jnp.max(score, axis=1, keepdims=True), own)
    yield
    score = jnp.exp(score - top)
    own = jnp.exp(own - top)
    total = jnp.sum(score, axis=1, keepdims=True) + own
    prob = (score / total).astype(BF16)
    own = (own / total).astype(BF16).astype(F32)
    yield
    for r in span:
        part = slice(r * heads, (r + 1) * heads)
        mixed = jnp.dot(prob[part], values_ref[r], preferred_element_type=F32)
        turn_ref[:, r, :] = mixed + own[part] * nv_ref[r : r + 1, :].astype(F32)
    yield
    for h in range(heads):
        out_ref[:, h * size : (h + 1) * size] = turn_ref[h].astype(BF16)


def stacked(rows_ref):
    pieces = [rows_ref[d].astype(F32) for d in range(rows_ref.shape[0])]
    return jnp.concatenate(pieces, axis=0).astype(BF16)


def gate_kernel(rows_ref, weight_ref, *refs):
    out_ref, context_ref, turn_ref = refs[6:]
    rows = stacked(rows_ref)
    steps = attention_steps(*refs[:6], context_ref, turn_ref)
    hidden = weight_ref.shape[1]
    width = next(n for n in (256, 256, hidden) if hidden % n == 0)
    for n in range(0, hidden, width):
        next(steps, None)
        out_ref[:, n : n + width] = jnp.dot(
            rows, weight_ref[:, n : n + width], preferred_element_type=F32
        )
    for _ in steps:
        pass


def gate_and_attend(came, weight, lengths, *operands):
    rows = came.shape[0] * CAP
    requests, heads, size = operands[0].shape
    return pl.pallas_call(
        gate_kernel,
        out_shape=(
            jax.ShapeDtypeStruct((rows, weight.shape[1]), F32),
            jax.ShapeDtypeStruct((requests, heads * size), BF16),
        ),
        in_specs=[VMEM] * 8,
        out_specs=(VMEM,) * 2,
        scratch_shapes=[pltpu.VMEM((heads, requests, size), F32)],
        compiler_params=params(4, rows),
        name="gate_and_attend",
    )(came, weight, lengths, *in_vmem(*operands))


def choose(owners_ref, routes_ref, weights_ref, picks_ref, weight_ref):
    tokens, width = picks_ref.shape
    eye = lax.broadcasted_iota(jnp.int32, (tokens, tokens), 0) == lax.broadcasted_iota(
        jnp.int32, (tokens, tokens), 1
    )
    rows = lax.broadcasted_iota(jnp.int32, (tokens, width), 0)
    slot = lax.broadcasted_iota(jnp.int32, (tokens, width), 1)
    ids = experts_of(owners_ref, slot // (width // EXPERTS))
    hit = jnp.zeros((tokens, width), F32)
    weight = jnp.zeros((tokens, 1), F32)
    for k in range(routes_ref.shape[0]):
        named = jnp.where(eye, routes_ref[k : k + 1, :], 0).sum(axis=1, keepdims=True)
        given = jnp.where(eye, weights_ref[k : k + 1, :], 0.0).sum(axis=1, keepdims=True)
        hit = jnp.where(named == ids, 1.0, hit)
        weight += jnp.where(named < EXPERTS, given, 0.0)
    rank = jnp.zeros((tokens, width), F32)
    for t in range(tokens - 1):
        rank += jnp.where(rows > t, hit[t : t + 1, :], 0.0)
    picks_ref[...] = jnp.where(rank == (slot % CAP).astype(F32), hit, 0.0).astype(BF16)
    weight_ref[...] = weight


def up_kernel(rows_ref, weight_ref, *refs):
    choose(*refs[:3], *refs[4:])
    refs[3][...] = jnp.dot(stacked(rows_ref), weight_ref[...], preferred_element_type=F32)


def up_and_choose(came, weight, owners, routes_t, weights_t):
    rows = came.shape[0] * CAP
    tokens = routes_t.shape[1]
    return pl.pallas_call(
        up_kernel,
        out_shape=(
            jax.ShapeDtypeStruct((rows, weight.shape[1]), F32),
            jax.ShapeDtypeStruct((tokens, rows), BF16),
            jax.ShapeDtypeStruct((tokens, 1), F32),
        ),
        in_specs=[VMEM] * 5,
        out_specs=(VMEM,) * 3,
        compiler_params=params(4, rows),
        name="up_and_choose",
    )(came, weight, owners, routes_t, weights_t)


def down_kernel(ga, gb, ua, ub, down_ref, out_ref):
    gate = ga[...] + gb[...]
    up = ua[...] + ub[...]
    hidden = (gate / (1.0 + jnp.exp(-gate)) * up).astype(BF16)
    total = jnp.dot(hidden, down_ref[...], preferred_element_type=F32)
    for d in range(out_ref.shape[0]):
        out_ref[d] = total[d * CAP : (d + 1) * CAP].astype(BF16)


def down(gate_pair, up_pair, w_down):
    rows = gate_pair[0].shape[0]
    return pl.pallas_call(
        down_kernel,
        out_shape=jax.ShapeDtypeStruct((rows // CAP, CAP, w_down.shape[1]), BF16),
        in_specs=[VMEM] * 5,
        out_specs=VMEM,
        compiler_params=params(2, rows),
        name="down",
    )(*gate_pair, *up_pair, w_down)


def combine_kernel(picks_ref, weight_ref, back_ref, out_ref):
    total = jnp.dot(picks_ref[...], stacked(back_ref), preferred_element_type=F32)
    out_ref[...] = (weight_ref[...] * total).astype(BF16)


def combine(picks, weight, back):
    devices, _, features = back.shape
    return pl.pallas_call(
        combine_kernel,
        out_shape=jax.ShapeDtypeStruct((picks.shape[0], features), BF16),
        in_specs=[VMEM] * 3,
        out_specs=VMEM,
        compiler_params=params(2, devices * CAP),
        name="combine",
    )(picks, weight, back)


def swap(x, axis, devices, mask):
    return lax.ppermute(x, axis, [(i, i ^ mask) for i in range(devices)])


def per_device(
    act_rows,
    routes,
    route_weights,
    owners,
    w_gate,
    w_up,
    w_down,
    queries,
    new_keys,
    new_values,
    key_cache,
    value_cache,
    lengths,
):
    devices = lax.axis_size("wide")
    group_size = devices // EXPERTS
    routes_t, weights_t = routes.T, route_weights.T
    w_gate, w_up, w_down = in_vmem(w_gate, w_up, w_down)
    owners, lengths = owners[None], lengths[None]
    picked = pick_rows(owners, routes_t, act_rows, group_size)
    came = lax.all_to_all(picked, "wide", split_axis=0, concat_axis=0, tiled=True)
    gate, context = gate_and_attend(
        came, w_gate, lengths, queries, new_keys, new_values, key_cache, value_cache
    )
    gate_pair = (gate, swap(gate, "narrow", 2, 1))
    up, picks, weight = up_and_choose(came, w_up, owners, routes_t, weights_t)
    up_pair = (up, swap(up, "narrow", 2, 1))
    partial_value = down(gate_pair, up_pair, w_down)
    back = lax.all_to_all(partial_value, "wide", split_axis=0, concat_axis=0, tiled=True)
    return (combine(picks, weight, back), context)


def solution(mesh):
    in_specs = (
        P(("groups", "wide"), "narrow"),
        P(("groups", "wide"), None),
        P(("groups", "wide"), None),
        P(),
        P("narrow", "wide"),
        P("narrow", "wide"),
        P("wide", "narrow"),
        P(("groups", "wide"), "narrow", None),
        P(("groups", "wide"), None),
        P(("groups", "wide"), None),
        P(("groups", "wide"), None, None),
        P(("groups", "wide"), None, None),
        P(("groups", "wide")),
    )
    out_specs = (P(("groups", "wide"), "narrow"), P(("groups", "wide"), "narrow"))
    return jax.shard_map(
        per_device, mesh=mesh, in_specs=in_specs, out_specs=out_specs, check_vma=False
    )
```

time: 133 us -> 37.1 us (0.28)
  blocking collectives: 59.4 us -> 24.5 us
  matrix products: 23.7 us -> 0 us
  waiting for transfers between devices: 23.3 us -> 1.03 us
  between operations: 14.2 us -> 0.93 us
  Pallas kernels: 0 us -> 9.83 us
  starting transfers between devices: 5.81 us -> 0.5 us
  local copies, waits for them, and re-layouts: 3.47 us -> 0.11 us
  other arithmetic: 2.56 us -> 0.01 us
    all_gather x2 -> x0, blocking collectives: 59.4 us -> none  [the longest x1 31.3 us: per_device(): lax.all_gather(act_rows, 'wide', axis=0, tiled=True)]
    all_to_all x0 -> x2, blocking collectives: none -> 24.5 us  [the longest x1 14.5 us: per_device(): lax.all_to_all(picked, 'wide', split_axis=0, concat_axis=0, tiled=True)]
    dot_general x9 -> x0, matrix products: 23.7 us -> none  [the longest x1 9.51 us: per_device(): gate_part = jnp.dot(flattened, w_gate, preferred_element_type=jnp.float32)]
    psum x1 -> x0, waiting for transfers between devices: 16 us -> none  [per_device(): gate_sum, up_sum = lax.psum((gate_part, up_part), 'narrow')]
    pallas_call x0 -> x5, Pallas kernels: none -> 9.83 us  [the longest x1 2.72 us: gate_and_attend(): pl.pallas_call(gate_kernel, out_shape=(jax.ShapeDtypeStruct((rows, weight...]
    all_to_all x1 -> x0, waiting for transfers between devices: 7.23 us -> none  [per_device(): lax.all_to_all(partial_value, 'wide', split_axis=0, concat_axis=0, tiled=...]
    all_to_all x1 -> x0, starting transfers between devices: 5.77 us -> none  [per_device(): lax.all_to_all(partial_value, 'wide', split_axis=0, concat_axis=0, tiled=...]
    unnamed x21 -> x40, local copies, waits for them, and re-layouts: 2.72 us -> 0.11 us
  transfers between devices with their start and end apart: 2 -> 2, of which waited for: 2 -> 1; matrix products, arithmetic and copies ran while one was open for 1% -> 0% of each run, Pallas kernels for 0% -> 7%
where the time goes in v3:
time: 37.1 us; the launch traced here: 36.9 us
  blocking collectives  24.5 us (66%)
  Pallas kernels  9.83 us (26%)
  waiting for transfers between devices  1.03 us (3%)
  between operations  0.93 us (3%)
  starting transfers between devices  0.5 us (1%)
    all_to_all x1, blocking collectives, per_device(): lax.all_to_all(picked, 'wide', split_axis=0, concat_axis=0, tiled=True)  14.5 us
    all_to_all x1, blocking collectives, per_device(): lax.all_to_all(partial_value, 'wide', split_axis=0, concat_axis=0, tiled=...  9.94 us
    pallas_call x1, Pallas kernels, gate_and_attend(): pl.pallas_call(gate_kernel, out_shape=(jax.ShapeDtypeStruct((rows, weight...  2.72 us
    pallas_call x1, Pallas kernels, up_and_choose(): pl.pallas_call(up_kernel, out_shape=(jax.ShapeDtypeStruct((rows, weight.s...  2.49 us
    pallas_call x1, Pallas kernels, down(): pl.pallas_call(down_kernel, out_shape=jax.ShapeDtypeStruct((rows // CAP,...  2.49 us
    pallas_call x1, Pallas kernels, pick_rows(): pl.pallas_call(functools.partial(pick_kernel, group_size), out_shape=jax....  1.31 us
    ppermute x2, waiting for transfers between devices, swap(): return lax.ppermute(x, axis, [(i, i ^ mask) for i in range(devices)])  1.03 us
    pallas_call x1, Pallas kernels, combine(): pl.pallas_call(combine_kernel, out_shape=jax.ShapeDtypeStruct((picks.shap...  0.82 us
  transfers between devices with their start and end apart: 2, of which 1 were waited for; matrix products, arithmetic and copies ran while one was open for 0% of the time, Pallas kernels for 7%

profile of v3, /device:TPU:0, one launch (start us, length us, event | category | flops | bytes accessed | tf_op | source)
XLA Modules:
  0.0 36.9 jit_solution(405447197964000596)
XLA Ops:
  0.6 0.0 slice-start
  0.7 0.0 slice-start.1
  0.7 0.0 slice-start.2
  0.7 0.0 slice-start.3
  0.7 0.0 slice-start.4
  0.8 1.3 %pick_rows.1 = bf16[8,2,3584]{2,1,0:T(2,128)(2,1)S(1)} custom-call(s32[1,4]{1,0:T(1,128)} %bitcast.11, s32[3,6]{1,0:T(4,128)} %bitcast.8, bf16[6,3584]{1,0:T(8,128)(2,1)} %act_hbm.1), custom_call_target="tpu_custom_call" | custom-call | flops 99999997952 | bytes 120000000 | tf_op jit(solution)/shard_map/pick_rows/pallas_call | solution.py:73
  2.1 0.0 copy-start.4
  2.1 0.0 copy-start.5
  2.1 0.0 copy-start.8
  2.1 14.5 %all_to_all.10.rows_ref = bf16[8,2,3584]{2,1,0:T(2,128)(2,1)S(1)} all-to-all(bf16[8,2,3584]{2,1,0:T(2,128)(2,1)S(1)} %pick_rows.1), channel_id=1, replica_groups=mesh['groups'=2,'wide'=8,'narrow'=2] {'wide'}, dimensions={0} | all-to-all | bytes 229376 | tf_op jit(solution)/shard_map/all_to_all | solution.py:274
  16.7 0.0 slice-start.5
  16.7 0.0 slice-start.6
  16.7 0.0 slice-start.7
  16.7 2.7 %gate_and_attend.1 = (f32[16,2560]{1,0:T(8,128)S(1)}, bf16[4,8192]{1,0:T(4,128)(2,1)}) custom-call(bf16[8,2,3584]{2,1,0:T(2,128)(2,1)S(1)} %all_to_all.10.rows_ref, bf16[3584,2560]{1,0:T(8,128)(2,1)S(1)} %copy-done, s32[1,4]{1,0:T(1,128)S(1)} %bitcast.13, bf16[4,32,256]{2,1,0:T(8,128)(2,1)S(1)} %copy-done.3, bf16[4,256]{1,0:T(4,128)(2,1)S(1)} %copy-done.6, ...), custom_call_target="tpu_custom_call" | custom-call | tf_op jit(solution)/shard_map/gate_and_attend/pallas_call | solution.py:153
  19.5 0.0 collective-permute-start
  19.5 0.0 slice-done
  19.6 0.0 slice-start.8
  19.6 0.0 slice-start.9
  19.6 2.5 %up_and_choose.1 = (f32[16,2560]{1,0:T(8,128)S(1)}, bf16[6,16]{1,0:T(8,128)(2,1)S(1)}, f32[6,1]{1,0:T(8,128)S(1)}) custom-call(bf16[8,2,3584]{2,1,0:T(2,128)(2,1)S(1)} %all_to_all.10.rows_ref, bf16[3584,2560]{1,0:T(8,128)(2,1)S(1)} %bitcast.5, s32[1,4]{1,0:T(1,128)S(1)} %bitcast.12, s32[3,6]{1,0:T(4,128)S(1)} %bitcast.9, f32[3,6]{1,0:T(4,128)S(1)} %bitcast.10), custom_call_target="tpu_custom_call" | custom-call | tf_op jit(solution)/shard_map/up_and_choose/pallas_call | solution.py:197
  22.1 0.5 %collective-permute-start.1 = (f32[16,2560]{1,0:T(8,128)S(1)}, f32[16,2560]{1,0:T(8,128)S(1)}, u32[]{:S(2)}, u32[]{:S(2)}) collective-permute-start(f32[16,2560]{1,0:T(8,128)S(1)} %get-tuple-element.10.ua), channel_id=1, source_target_pairs={{0,1},{1,0},{2,3},{3,2},{4,5},{5,4},{6,7},{7,6},{8,9},{9,8},{10,11... | collective-permute-start | bytes 491528 | tf_op jit(solution)/shard_map/ppermute | solution.py:250
  22.6 1.0 %collective-permute-done.1.ub = f32[16,2560]{1,0:T(8,128)S(1)} collective-permute-done((f32[16,2560]{1,0:T(8,128)S(1)}, f32[16,2560]{1,0:T(8,128)S(1)}, u32[]{:S(2)}, u32[]{:S(2)}) %collective-permute-start.1) | collective-permute-done | bytes 163872 | tf_op jit(solution)/shard_map/ppermute | solution.py:250
  23.6 2.5 %down.1 = bf16[8,2,3584]{2,1,0:T(2,128)(2,1)S(1)} custom-call(f32[16,2560]{1,0:T(8,128)S(1)} %get-tuple-element.9.ga, f32[16,2560]{1,0:T(8,128)S(1)} %collective-permute-done.gb, f32[16,2560]{1,0:T(8,128)S(1)} %get-tuple-element.10.ua, f32[16,2560]{1,0:T(8,128)S(1)} %collective-permute-done.1.ub, bf16[2560,3584]{1,0:T(8,128)(2,1)S(1)} %bitcast.7), custom_call_target="tpu_custom_call" | custom-call | tf_op jit(solution)/shard_map/down/pallas_call | solution.py:222
  26.1 9.9 %all_to_all.11.back_ref = bf16[8,2,3584]{2,1,0:T(2,128)(2,1)S(1)} all-to-all(bf16[8,2,3584]{2,1,0:T(2,128)(2,1)S(1)} %down.1), channel_id=1, replica_groups=mesh['groups'=2,'wide'=8,'narrow'=2] {'wide'}, dimensions={0} | all-to-all | bytes 229376 | tf_op jit(solution)/shard_map/all_to_all | solution.py:282
  36.1 0.8 %combine.1 = bf16[6,3584]{1,0:T(8,128)(2,1)} custom-call(bf16[6,16]{1,0:T(8,128)(2,1)S(1)} %get-tuple-element.7.picks_ref, f32[6,1]{1,0:T(8,128)S(1)} %get-tuple-element.8.weight_ref, bf16[8,2,3584]{2,1,0:T(2,128)(2,1)S(1)} %all_to_all.11.back_ref), custom_call_target="tpu_custom_call" | custom-call | tf_op jit(solution)/shard_map/combine/pallas_call | solution.py:239
  (29 shorter events, 0.1 us)
Async XLA Ops:
  0.6 18.8 %slice-start = ((s8[18350080]{0:T(1024)(128)(4,1)}), s8[4194304]{0:T(1024)(128)(4,1)S(1)}, s32[]{:S(2)}) async-start(s8[18350080]{0:T(1024)(128)(4,1)} %bitcast.4), calls=%async_computation.2 | async-start | bytes 8388608
  0.6 16.0 %copy-start = (bf16[3584,2560]{1,0:T(8,128)(2,1)S(1)}, bf16[3584,2560]{1,0:T(8,128)(2,1)}, u32[]{:S(2)}) copy-start(bf16[3584,2560]{1,0:T(8,128)(2,1)} %weight_ref.3) | copy-start | bytes 55050244
  0.7 16.0 %copy-start.1 = (bf16[4,256,256]{2,1,0:T(8,128)(2,1)S(1)}, bf16[4,256,256]{2,1,0:T(8,128)(2,1)}, u32[]{:S(2)}) copy-start(bf16[4,256,256]{2,1,0:T(8,128)(2,1)} %refs_4_.1) | copy-start | bytes 1572868
  0.7 16.0 %copy-start.2 = (bf16[4,256,256]{2,1,0:T(8,128)(2,1)S(1)}, bf16[4,256,256]{2,1,0:T(8,128)(2,1)}, u32[]{:S(2)}) copy-start(bf16[4,256,256]{2,1,0:T(8,128)(2,1)} %refs_5_.1) | copy-start | bytes 1572868
  0.7 16.0 %copy-start.3 = (bf16[4,32,256]{2,1,0:T(8,128)(2,1)S(1)}, bf16[4,32,256]{2,1,0:T(8,128)(2,1)}, u32[]{:S(2)}) copy-start(bf16[4,32,256]{2,1,0:T(8,128)(2,1)} %refs_1_.1) | copy-start | bytes 196612
  0.7 16.0 %copy-start.6 = (bf16[4,256]{1,0:T(4,128)(2,1)S(1)}, bf16[4,256]{1,0:T(4,128)(2,1)}, u32[]{:S(2)}) copy-start(bf16[4,256]{1,0:T(4,128)(2,1)} %refs_2_.1) | copy-start | bytes 6148
  0.7 16.0 %copy-start.7 = (bf16[4,256]{1,0:T(4,128)(2,1)S(1)}, bf16[4,256]{1,0:T(4,128)(2,1)}, u32[]{:S(2)}) copy-start(bf16[4,256]{1,0:T(4,128)(2,1)} %refs_3_.1) | copy-start | bytes 6148
  0.7 16.0 %copy-start.9 = (s32[4]{0:T(128)S(1)}, s32[4]{0:T(128)}, u32[]{:S(2)}) copy-start(s32[4]{0:T(128)} %param.25) | copy-start | bytes 52
  0.7 18.8 %slice-start.1 = ((s8[18350080]{0:T(1024)(128)(4,1)}), s8[4194304]{0:T(1024)(128)(4,1)S(1)}, s32[]{:S(2)}) async-start(s8[18350080]{0:T(1024)(128)(4,1)} %bitcast.4), calls=%async_computation.3 | async-start | bytes 8388608
  0.7 18.8 %slice-start.2 = ((s8[18350080]{0:T(1024)(128)(4,1)}), s8[4194304]{0:T(1024)(128)(4,1)S(1)}, s32[]{:S(2)}) async-start(s8[18350080]{0:T(1024)(128)(4,1)} %bitcast.4), calls=%async_computation.4 | async-start | bytes 8388608
  0.7 18.8 %slice-start.3 = ((s8[18350080]{0:T(1024)(128)(4,1)}), s8[4194304]{0:T(1024)(128)(4,1)S(1)}, s32[]{:S(2)}) async-start(s8[18350080]{0:T(1024)(128)(4,1)} %bitcast.4), calls=%async_computation.5 | async-start | bytes 8388608
  0.7 18.8 %slice-start.4 = ((s8[18350080]{0:T(1024)(128)(4,1)}), s8[1572864]{0:T(1024)(128)(4,1)S(1)}, s32[]{:S(2)}) async-start(s8[18350080]{0:T(1024)(128)(4,1)} %bitcast.4), calls=%async_computation.6 | async-start | bytes 3145728
  2.1 17.5 %copy-start.4 = (s32[6,3]{0,1:T(4,128)S(1)}, s32[6,3]{0,1:T(4,128)}, u32[]{:S(2)}) copy-start(s32[6,3]{0,1:T(4,128)} %param.14) | copy-start | bytes 220
  2.1 17.5 %copy-start.5 = (f32[6,3]{0,1:T(4,128)S(1)}, f32[6,3]{0,1:T(4,128)}, u32[]{:S(2)}) copy-start(f32[6,3]{0,1:T(4,128)} %param.15) | copy-start | bytes 220
  2.1 17.5 %copy-start.8 = (s32[4]{0:T(128)S(1)}, s32[4]{0:T(128)}, u32[]{:S(2)}) copy-start(s32[4]{0:T(128)} %param.16) | copy-start | bytes 52
  16.7 6.9 %slice-start.5 = ((s8[18350080]{0:T(1024)(128)(4,1)}), s8[4194304]{0:T(1024)(128)(4,1)S(1)}, s32[]{:S(2)}) async-start(s8[18350080]{0:T(1024)(128)(4,1)} %bitcast.6), calls=%async_computation.7 | async-start | bytes 8388608
  16.7 6.9 %slice-start.6 = ((s8[18350080]{0:T(1024)(128)(4,1)}), s8[4194304]{0:T(1024)(128)(4,1)S(1)}, s32[]{:S(2)}) async-start(s8[18350080]{0:T(1024)(128)(4,1)} %bitcast.6), calls=%async_computation.8 | async-start | bytes 8388608
  16.7 6.9 %slice-start.7 = ((s8[18350080]{0:T(1024)(128)(4,1)}), s8[4194304]{0:T(1024)(128)(4,1)S(1)}, s32[]{:S(2)}) async-start(s8[18350080]{0:T(1024)(128)(4,1)} %bitcast.6), calls=%async_computation.9 | async-start | bytes 8388608
  19.5 3.1 %collective-permute-start = (f32[16,2560]{1,0:T(8,128)S(1)}, f32[16,2560]{1,0:T(8,128)S(1)}, u32[]{:S(2)}, u32[]{:S(2)}) collective-permute-start(f32[16,2560]{1,0:T(8,128)S(1)} %get-tuple-element.9.ga), channel_id=1, source_target_pairs={{0,1},{1,0},{2,3},{3,2},{4,5},{5,4},{6,7},{7,6},{8,9},{9,8},{10,11... | collective-permute-start | bytes 491528 | tf_op jit(solution)/shard_map/ppermute | solution.py:250
  19.6 4.0 %slice-start.8 = ((s8[18350080]{0:T(1024)(128)(4,1)}), s8[4194304]{0:T(1024)(128)(4,1)S(1)}, s32[]{:S(2)}) async-start(s8[18350080]{0:T(1024)(128)(4,1)} %bitcast.6), calls=%async_computation.10 | async-start | bytes 8388608
  19.6 4.0 %slice-start.9 = ((s8[18350080]{0:T(1024)(128)(4,1)}), s8[1572864]{0:T(1024)(128)(4,1)S(1)}, s32[]{:S(2)}) async-start(s8[18350080]{0:T(1024)(128)(4,1)} %bitcast.6), calls=%async_computation.11 | async-start | bytes 3145728
  22.1 1.5 %collective-permute-start.1 = (f32[16,2560]{1,0:T(8,128)S(1)}, f32[16,2560]{1,0:T(8,128)S(1)}, u32[]{:S(2)}, u32[]{:S(2)}) collective-permute-start(f32[16,2560]{1,0:T(8,128)S(1)} %get-tuple-element.10.ua), channel_id=1, source_target_pairs={{0,1},{1,0},{2,3},{3,2},{4,5},{5,4},{6,7},{7,6},{8,9},{9,8},{10,11... | collective-permute-start | bytes 491528 | tf_op jit(solution)/shard_map/ppermute | solution.py:250

commit v4 on v3

--- a/solution.py
+++ b/solution.py
@@ -50,7 +50,7 @@
     copies = fetch(
         ((owners_hbm, owners_ref), (routes_hbm, routes_ref), (act_hbm, act_ref)), sems
     )
-    for copy in copies:
+    for copy in copies[:2]:
         copy.wait()
     tokens = act_ref.shape[0]
     rows = lax.broadcasted_iota(jnp.int32, (SLOTS, tokens), 0)
@@ -63,6 +63,7 @@
     for t in range(tokens - 1):
         rank += jnp.where(cols > t, hit[:, t : t + 1], 0.0)
     picks = jnp.where(rank == (rows % CAP).astype(F32), hit, 0.0).astype(BF16)
+    copies[2].wait()
     chosen = jnp.dot(picks, act_ref[...], preferred_element_type=F32)
     for m in range(EXPERTS):
         for j in range(group_size):
@@ -132,9 +133,10 @@
     return jnp.concatenate(pieces, axis=0).astype(BF16)
 
 
-def gate_kernel(rows_ref, weight_ref, *refs):
-    out_ref, context_ref, turn_ref = refs[6:]
-    rows = stacked(rows_ref)
+def gate_kernel(came_ref, weight_ref, *refs):
+    out_ref, rows_ref, context_ref, turn_ref = refs[6:]
+    rows = stacked(came_ref)
+    rows_ref[...] = rows
     steps = attention_steps(*refs[:6], context_ref, turn_ref)
     hidden = weight_ref.shape[1]
     width = next(n for n in (256, 256, hidden) if hidden % n == 0)
@@ -154,10 +156,11 @@
         gate_kernel,
         out_shape=(
             jax.ShapeDtypeStruct((rows, weight.shape[1]), F32),
+            jax.ShapeDtypeStruct((rows, weight.shape[0]), BF16),
             jax.ShapeDtypeStruct((requests, heads * size), BF16),
         ),
         in_specs=[VMEM] * 8,
-        out_specs=(VMEM,) * 2,
+        out_specs=(VMEM,) * 3,
         scratch_shapes=[pltpu.VMEM((heads, requests, size), F32)],
         compiler_params=params(4, rows),
         name="gate_and_attend",
@@ -186,47 +189,48 @@
     weight_ref[...] = weight
 
 
-def up_kernel(rows_ref, weight_ref, *refs):
+def up_kernel(rows_ref, weight_ref, gate_ref, *refs):
     choose(*refs[:3], *refs[4:])
-    refs[3][...] = jnp.dot(stacked(rows_ref), weight_ref[...], preferred_element_type=F32)
-
-
-def up_and_choose(came, weight, owners, routes_t, weights_t):
-    rows = came.shape[0] * CAP
+    refs[3][0] = gate_ref[...]
+    refs[3][1] = jnp.dot(rows_ref[...], weight_ref[...], preferred_element_type=F32)
+
+
+def up_and_choose(came_rows, weight, gate, owners, routes_t, weights_t):
+    rows = came_rows.shape[0]
     tokens = routes_t.shape[1]
     return pl.pallas_call(
         up_kernel,
         out_shape=(
-            jax.ShapeDtypeStruct((rows, weight.shape[1]), F32),
+            jax.ShapeDtypeStruct((2, rows, weight.shape[1]), F32),
             jax.ShapeDtypeStruct((tokens, rows), BF16),
             jax.ShapeDtypeStruct((tokens, 1), F32),
         ),
-        in_specs=[VMEM] * 5,
+        in_specs=[VMEM] * 6,
         out_specs=(VMEM,) * 3,
         compiler_params=params(4, rows),
         name="up_and_choose",
-    )(came, weight, owners, routes_t, weights_t)
-
-
-def down_kernel(ga, gb, ua, ub, down_ref, out_ref):
-    gate = ga[...] + gb[...]
-    up = ua[...] + ub[...]
+    )(came_rows, weight, gate, owners, routes_t, weights_t)
+
+
+def down_kernel(here_ref, there_ref, down_ref, out_ref):
+    gate = here_ref[0] + there_ref[0]
+    up = here_ref[1] + there_ref[1]
     hidden = (gate / (1.0 + jnp.exp(-gate)) * up).astype(BF16)
     total = jnp.dot(hidden, down_ref[...], preferred_element_type=F32)
     for d in range(out_ref.shape[0]):
         out_ref[d] = total[d * CAP : (d + 1) * CAP].astype(BF16)
 
 
-def down(gate_pair, up_pair, w_down):
-    rows = gate_pair[0].shape[0]
+def down(here, there, w_down):
+    rows = here.shape[1]
     return pl.pallas_call(
         down_kernel,
         out_shape=jax.ShapeDtypeStruct((rows // CAP, CAP, w_down.shape[1]), BF16),
-        in_specs=[VMEM] * 5,
+        in_specs=[VMEM] * 3,
         out_specs=VMEM,
         compiler_params=params(2, rows),
         name="down",
-    )(*gate_pair, *up_pair, w_down)
+    )(here, there, w_down)
 
 
 def combine_kernel(picks_ref, weight_ref, back_ref, out_ref):
@@ -272,13 +276,11 @@
     owners, lengths = owners[None], lengths[None]
     picked = pick_rows(owners, routes_t, act_rows, group_size)
     came = lax.all_to_all(picked, "wide", split_axis=0, concat_axis=0, tiled=True)
-    gate, context = gate_and_attend(
+    gate, came_rows, context = gate_and_attend(
         came, w_gate, lengths, queries, new_keys, new_values, key_cache, value_cache
     )
-    gate_pair = (gate, swap(gate, "narrow", 2, 1))
-    up, picks, weight = up_and_choose(came, w_up, owners, routes_t, weights_t)
-    up_pair = (up, swap(up, "narrow", 2, 1))
-    partial_value = down(gate_pair, up_pair, w_down)
+    sums, picks, weight = up_and_choose(came_rows, w_up, gate, owners, routes_t, weights_t)
+    partial_value = down(sums, swap(sums, "narrow", 2, 1), w_down)
     back = lax.all_to_all(partial_value, "wide", split_axis=0, concat_axis=0, tiled=True)
     return (combine(picks, weight, back), context)
 

time: 37.1 us -> 36.8 us (level)
  waiting for transfers between devices: 1.03 us -> 1.63 us
  starting transfers between devices: 0.5 us -> 0.01 us
    ppermute x2 -> x1, waiting for transfers between devices: 1.03 us -> 1.63 us  [swap(): return lax.ppermute(x, axis, [(i, i ^ mask) for i in range(devices)])]
    ppermute x2 -> x1, starting transfers between devices: 0.5 us -> 0.01 us  [swap(): return lax.ppermute(x, axis, [(i, i ^ mask) for i in range(devices)])]
  transfers between devices with their start and end apart: 2 -> 1, of which waited for: 1 -> 1; matrix products, arithmetic and copies ran while one was open for 0% -> 0% of each run, Pallas kernels for 7% -> 0%
where the time goes in v4:
time: 36.8 us; the launch traced here: 36.6 us
  blocking collectives  24.2 us (66%)
  Pallas kernels  9.69 us (26%)
  waiting for transfers between devices  1.63 us (4%)
  between operations  0.93 us (3%)
    all_to_all x1, blocking collectives, per_device(): lax.all_to_all(picked, 'wide', split_axis=0, concat_axis=0, tiled=True)  14.5 us
    all_to_all x1, blocking collectives, per_device(): lax.all_to_all(partial_value, 'wide', split_axis=0, concat_axis=0, tiled=...  9.7 us
    pallas_call x1, Pallas kernels, gate_and_attend(): pl.pallas_call(gate_kernel, out_shape=(jax.ShapeDtypeStruct((rows, weight...  2.72 us
    pallas_call x1, Pallas kernels, down(): pl.pallas_call(down_kernel, out_shape=jax.ShapeDtypeStruct((rows // CAP,...  2.49 us
    pallas_call x1, Pallas kernels, up_and_choose(): pl.pallas_call(up_kernel, out_shape=(jax.ShapeDtypeStruct((2, rows, weigh...  2.48 us
    ppermute x1, waiting for transfers between devices, swap(): return lax.ppermute(x, axis, [(i, i ^ mask) for i in range(devices)])  1.63 us
    pallas_call x1, Pallas kernels, pick_rows(): pl.pallas_call(functools.partial(pick_kernel, group_size), out_shape=jax....  1.17 us
    pallas_call x1, Pallas kernels, combine(): pl.pallas_call(combine_kernel, out_shape=jax.ShapeDtypeStruct((picks.shap...  0.82 us
  transfers between devices with their start and end apart: 1, of which 1 were waited for; matrix products, arithmetic and copies ran while one was open for 0% of the time, Pallas kernels for 0%

profile of v4, /device:TPU:0, one launch (start us, length us, event | category | flops | bytes accessed | tf_op | source)
XLA Modules:
  0.0 36.6 jit_solution(11762671960668000404)
XLA Ops:
  0.6 0.0 slice-start
  0.7 0.0 slice-start.1
  0.7 0.0 slice-start.2
  0.7 0.0 slice-start.3
  0.7 0.0 slice-start.4
  0.8 1.2 %pick_rows.1 = bf16[8,2,3584]{2,1,0:T(2,128)(2,1)S(1)} custom-call(s32[1,4]{1,0:T(1,128)} %bitcast.12, s32[3,6]{1,0:T(4,128)} %bitcast.8, bf16[6,3584]{1,0:T(8,128)(2,1)} %act_hbm.1), custom_call_target="tpu_custom_call" | custom-call | flops 99999997952 | bytes 120000000 | tf_op jit(solution)/shard_map/pick_rows/pallas_call | solution.py:74
  1.9 0.0 copy-start.6
  1.9 0.0 copy-start.7
  2.0 0.0 copy-start.9
  2.0 14.5 %all_to_all.10.came_ref = bf16[8,2,3584]{2,1,0:T(2,128)(2,1)S(1)} all-to-all(bf16[8,2,3584]{2,1,0:T(2,128)(2,1)S(1)} %pick_rows.1), channel_id=1, replica_groups=mesh['groups'=2,'wide'=8,'narrow'=2] {'wide'}, dimensions={0} | all-to-all | bytes 229376 | tf_op jit(solution)/shard_map/all_to_all | solution.py:278
  16.6 0.0 slice-start.5
  16.6 0.0 slice-start.6
  16.6 0.0 slice-start.7
  16.6 2.7 %gate_and_attend.1 = (f32[16,2560]{1,0:T(8,128)S(1)}, bf16[16,3584]{1,0:T(8,128)(2,1)S(1)}, bf16[4,8192]{1,0:T(4,128)(2,1)}) custom-call(bf16[8,2,3584]{2,1,0:T(2,128)(2,1)S(1)} %all_to_all.10.came_ref, bf16[3584,2560]{1,0:T(8,128)(2,1)S(1)} %copy-done, s32[1,4]{1,0:T(1,128)S(1)} %bitcast.11, bf16[4,32,256]{2,1,0:T(8,128)(2,1)S(1)} %copy-done.3, ...), custom_call_target="tpu_custom_call" | custom-call | tf_op jit(solution)/shard_map/gate_and_attend/pallas_call | solution.py:155
  19.3 0.0 slice-done.2
  19.4 0.0 slice-start.8
  19.4 0.0 slice-start.9
  19.4 2.5 %up_and_choose.1 = (f32[2,16,2560]{2,1,0:T(8,128)S(1)}, bf16[6,16]{1,0:T(8,128)(2,1)S(1)}, f32[6,1]{1,0:T(8,128)S(1)}) custom-call(bf16[16,3584]{1,0:T(8,128)(2,1)S(1)} %get-tuple-element.8.rows_ref, bf16[3584,2560]{1,0:T(8,128)(2,1)S(1)} %bitcast.5, f32[16,2560]{1,0:T(8,128)S(1)} %get-tuple-element.9.gate_ref, s32[1,4]{1,0:T(1,128)S(1)} %bitcast.13, ...), custom_call_target="tpu_custom_call" | custom-call | tf_op jit(solution)/shard_map/up_and_choose/pallas_call | solution.py:201
  21.9 0.0 collective-permute-start
  21.9 1.6 %collective-permute-done.there_ref = f32[2,16,2560]{2,1,0:T(8,128)S(1)} collective-permute-done((f32[2,16,2560]{2,1,0:T(8,128)S(1)}, f32[2,16,2560]{2,1,0:T(8,128)S(1)}, u32[]{:S(2)}, u32[]{:S(2)}) %collective-permute-start) | collective-permute-done | bytes 327712 | tf_op jit(solution)/shard_map/ppermute | solution.py:254
  23.6 0.0 slice-done.5
  23.6 2.5 %down.1 = bf16[8,2,3584]{2,1,0:T(2,128)(2,1)S(1)} custom-call(f32[2,16,2560]{2,1,0:T(8,128)S(1)} %get-tuple-element.12.here_ref, f32[2,16,2560]{2,1,0:T(8,128)S(1)} %collective-permute-done.there_ref, bf16[2560,3584]{1,0:T(8,128)(2,1)S(1)} %bitcast.7), custom_call_target="tpu_custom_call" | custom-call | tf_op jit(solution)/shard_map/down/pallas_call | solution.py:226
  26.1 9.7 %all_to_all.11.back_ref = bf16[8,2,3584]{2,1,0:T(2,128)(2,1)S(1)} all-to-all(bf16[8,2,3584]{2,1,0:T(2,128)(2,1)S(1)} %down.1), channel_id=1, replica_groups=mesh['groups'=2,'wide'=8,'narrow'=2] {'wide'}, dimensions={0} | all-to-all | bytes 229376 | tf_op jit(solution)/shard_map/all_to_all | solution.py:284
  35.8 0.8 %combine.1 = bf16[6,3584]{1,0:T(8,128)(2,1)} custom-call(bf16[6,16]{1,0:T(8,128)(2,1)S(1)} %get-tuple-element.10.picks_ref, f32[6,1]{1,0:T(8,128)S(1)} %get-tuple-element.11.weight_ref, bf16[8,2,3584]{2,1,0:T(2,128)(2,1)S(1)} %all_to_all.11.back_ref), custom_call_target="tpu_custom_call" | custom-call | tf_op jit(solution)/shard_map/combine/pallas_call | solution.py:243
  (27 shorter events, 0.1 us)
Async XLA Ops:
  0.6 18.7 %slice-start = ((s8[18350080]{0:T(1024)(128)(4,1)}), s8[4194304]{0:T(1024)(128)(4,1)S(1)}, s32[]{:S(2)}) async-start(s8[18350080]{0:T(1024)(128)(4,1)} %bitcast.4), calls=%async_computation.2 | async-start | bytes 8388608
  0.6 15.9 %copy-start = (bf16[3584,2560]{1,0:T(8,128)(2,1)S(1)}, bf16[3584,2560]{1,0:T(8,128)(2,1)}, u32[]{:S(2)}) copy-start(bf16[3584,2560]{1,0:T(8,128)(2,1)} %weight_ref.2) | copy-start | bytes 55050244
  0.7 15.9 %copy-start.1 = (bf16[4,256,256]{2,1,0:T(8,128)(2,1)S(1)}, bf16[4,256,256]{2,1,0:T(8,128)(2,1)}, u32[]{:S(2)}) copy-start(bf16[4,256,256]{2,1,0:T(8,128)(2,1)} %refs_4_.1) | copy-start | bytes 1572868
  0.7 15.9 %copy-start.2 = (bf16[4,256,256]{2,1,0:T(8,128)(2,1)S(1)}, bf16[4,256,256]{2,1,0:T(8,128)(2,1)}, u32[]{:S(2)}) copy-start(bf16[4,256,256]{2,1,0:T(8,128)(2,1)} %refs_5_.1) | copy-start | bytes 1572868
  0.7 15.9 %copy-start.3 = (bf16[4,32,256]{2,1,0:T(8,128)(2,1)S(1)}, bf16[4,32,256]{2,1,0:T(8,128)(2,1)}, u32[]{:S(2)}) copy-start(bf16[4,32,256]{2,1,0:T(8,128)(2,1)} %refs_1_.1) | copy-start | bytes 196612
  0.7 15.9 %copy-start.4 = (bf16[4,256]{1,0:T(4,128)(2,1)S(1)}, bf16[4,256]{1,0:T(4,128)(2,1)}, u32[]{:S(2)}) copy-start(bf16[4,256]{1,0:T(4,128)(2,1)} %refs_2_.1) | copy-start | bytes 6148
  0.7 15.9 %copy-start.5 = (bf16[4,256]{1,0:T(4,128)(2,1)S(1)}, bf16[4,256]{1,0:T(4,128)(2,1)}, u32[]{:S(2)}) copy-start(bf16[4,256]{1,0:T(4,128)(2,1)} %refs_3_.1) | copy-start | bytes 6148
  0.7 15.9 %copy-start.8 = (s32[4]{0:T(128)S(1)}, s32[4]{0:T(128)}, u32[]{:S(2)}) copy-start(s32[4]{0:T(128)} %param.25) | copy-start | bytes 52
  0.7 18.6 %slice-start.1 = ((s8[18350080]{0:T(1024)(128)(4,1)}), s8[4194304]{0:T(1024)(128)(4,1)S(1)}, s32[]{:S(2)}) async-start(s8[18350080]{0:T(1024)(128)(4,1)} %bitcast.4), calls=%async_computation.3 | async-start | bytes 8388608
  0.7 18.6 %slice-start.2 = ((s8[18350080]{0:T(1024)(128)(4,1)}), s8[4194304]{0:T(1024)(128)(4,1)S(1)}, s32[]{:S(2)}) async-start(s8[18350080]{0:T(1024)(128)(4,1)} %bitcast.4), calls=%async_computation.4 | async-start | bytes 8388608
  0.7 18.6 %slice-start.3 = ((s8[18350080]{0:T(1024)(128)(4,1)}), s8[4194304]{0:T(1024)(128)(4,1)S(1)}, s32[]{:S(2)}) async-start(s8[18350080]{0:T(1024)(128)(4,1)} %bitcast.4), calls=%async_computation.5 | async-start | bytes 8388608
  0.7 18.6 %slice-start.4 = ((s8[18350080]{0:T(1024)(128)(4,1)}), s8[1572864]{0:T(1024)(128)(4,1)S(1)}, s32[]{:S(2)}) async-start(s8[18350080]{0:T(1024)(128)(4,1)} %bitcast.4), calls=%async_computation.6 | async-start | bytes 3145728
  1.9 17.4 %copy-start.6 = (s32[6,3]{0,1:T(4,128)S(1)}, s32[6,3]{0,1:T(4,128)}, u32[]{:S(2)}) copy-start(s32[6,3]{0,1:T(4,128)} %param.14) | copy-start | bytes 220
  1.9 17.4 %copy-start.7 = (f32[6,3]{0,1:T(4,128)S(1)}, f32[6,3]{0,1:T(4,128)}, u32[]{:S(2)}) copy-start(f32[6,3]{0,1:T(4,128)} %param.15) | copy-start | bytes 220
  2.0 17.4 %copy-start.9 = (s32[4]{0:T(128)S(1)}, s32[4]{0:T(128)}, u32[]{:S(2)}) copy-start(s32[4]{0:T(128)} %param.16) | copy-start | bytes 52
  16.6 7.0 %slice-start.5 = ((s8[18350080]{0:T(1024)(128)(4,1)}), s8[4194304]{0:T(1024)(128)(4,1)S(1)}, s32[]{:S(2)}) async-start(s8[18350080]{0:T(1024)(128)(4,1)} %bitcast.6), calls=%async_computation.7 | async-start | bytes 8388608
  16.6 7.0 %slice-start.6 = ((s8[18350080]{0:T(1024)(128)(4,1)}), s8[4194304]{0:T(1024)(128)(4,1)S(1)}, s32[]{:S(2)}) async-start(s8[18350080]{0:T(1024)(128)(4,1)} %bitcast.6), calls=%async_computation.8 | async-start | bytes 8388608
  16.6 7.0 %slice-start.7 = ((s8[18350080]{0:T(1024)(128)(4,1)}), s8[4194304]{0:T(1024)(128)(4,1)S(1)}, s32[]{:S(2)}) async-start(s8[18350080]{0:T(1024)(128)(4,1)} %bitcast.6), calls=%async_computation.9 | async-start | bytes 8388608
  19.4 4.2 %slice-start.8 = ((s8[18350080]{0:T(1024)(128)(4,1)}), s8[4194304]{0:T(1024)(128)(4,1)S(1)}, s32[]{:S(2)}) async-start(s8[18350080]{0:T(1024)(128)(4,1)} %bitcast.6), calls=%async_computation.10 | async-start | bytes 8388608
  19.4 4.1 %slice-start.9 = ((s8[18350080]{0:T(1024)(128)(4,1)}), s8[1572864]{0:T(1024)(128)(4,1)S(1)}, s32[]{:S(2)}) async-start(s8[18350080]{0:T(1024)(128)(4,1)} %bitcast.6), calls=%async_computation.11 | async-start | bytes 3145728
  21.9 1.6 %collective-permute-start = (f32[2,16,2560]{2,1,0:T(8,128)S(1)}, f32[2,16,2560]{2,1,0:T(8,128)S(1)}, u32[]{:S(2)}, u32[]{:S(2)}) collective-permute-start(f32[2,16,2560]{2,1,0:T(8,128)S(1)} %get-tuple-element.12.here_ref), channel_id=1, source_target_pairs={{0,1},{1,0},{2,3},{3,2},{4,5},{5,4},{6,7},{7,6},{8,9},{9,8},{10,11... | collective-permute-start | bytes 983048 | tf_op jit(solution)/shard_map/ppermute | solution.py:254

commit v5 on v4

--- a/solution.py
+++ b/solution.py
@@ -190,9 +190,14 @@
 
 
 def up_kernel(rows_ref, weight_ref, gate_ref, *refs):
-    choose(*refs[:3], *refs[4:])
-    refs[3][0] = gate_ref[...]
-    refs[3][1] = jnp.dot(rows_ref[...], weight_ref[...], preferred_element_type=F32)
+    own_ref, sent_ref = refs[3:5]
+    choose(*refs[:3], *refs[5:])
+    gate = gate_ref[...]
+    own_ref[0] = gate
+    sent_ref[0] = gate.astype(BF16)
+    up = jnp.dot(rows_ref[...], weight_ref[...], preferred_element_type=F32)
+    own_ref[1] = up
+    sent_ref[1] = up.astype(BF16)
 
 
 def up_and_choose(came_rows, weight, gate, owners, routes_t, weights_t):
@@ -202,19 +207,20 @@
         up_kernel,
         out_shape=(
             jax.ShapeDtypeStruct((2, rows, weight.shape[1]), F32),
+            jax.ShapeDtypeStruct((2, rows, weight.shape[1]), BF16),
             jax.ShapeDtypeStruct((tokens, rows), BF16),
             jax.ShapeDtypeStruct((tokens, 1), F32),
         ),
         in_specs=[VMEM] * 6,
-        out_specs=(VMEM,) * 3,
+        out_specs=(VMEM,) * 4,
         compiler_params=params(4, rows),
         name="up_and_choose",
     )(came_rows, weight, gate, owners, routes_t, weights_t)
 
 
 def down_kernel(here_ref, there_ref, down_ref, out_ref):
-    gate = here_ref[0] + there_ref[0]
-    up = here_ref[1] + there_ref[1]
+    gate = here_ref[0] + there_ref[0].astype(F32)
+    up = here_ref[1] + there_ref[1].astype(F32)
     hidden = (gate / (1.0 + jnp.exp(-gate)) * up).astype(BF16)
     total = jnp.dot(hidden, down_ref[...], preferred_element_type=F32)
     for d in range(out_ref.shape[0]):
@@ -279,8 +285,10 @@
     gate, came_rows, context = gate_and_attend(
         came, w_gate, lengths, queries, new_keys, new_values, key_cache, value_cache
     )
-    sums, picks, weight = up_and_choose(came_rows, w_up, gate, owners, routes_t, weights_t)
-    partial_value = down(sums, swap(sums, "narrow", 2, 1), w_down)
+    own, sent, picks, weight = up_and_choose(
+        came_rows, w_up, gate, owners, routes_t, weights_t
+    )
+    partial_value = down(own, swap(sent, "narrow", 2, 1), w_down)
     back = lax.all_to_all(partial_value, "wide", split_axis=0, concat_axis=0, tiled=True)
     return (combine(picks, weight, back), context)
 

time: 36.8 us -> 36.6 us (level)
  no operation moved by 1% of the time
where the time goes in v5:
time: 36.6 us; the launch traced here: 36.4 us
  blocking collectives  24.3 us (66%)
  Pallas kernels  9.7 us (27%)
  waiting for transfers between devices  1.4 us (4%)
  between operations  0.93 us (3%)
    all_to_all x1, blocking collectives, per_device(): lax.all_to_all(picked, 'wide', split_axis=0, concat_axis=0, tiled=True)  14.5 us
    all_to_all x1, blocking collectives, per_device(): lax.all_to_all(partial_value, 'wide', split_axis=0, concat_axis=0, tiled=...  9.71 us
    pallas_call x1, Pallas kernels, gate_and_attend(): pl.pallas_call(gate_kernel, out_shape=(jax.ShapeDtypeStruct((rows, weight...  2.72 us
    pallas_call x1, Pallas kernels, down(): pl.pallas_call(down_kernel, out_shape=jax.ShapeDtypeStruct((rows // CAP,...  2.49 us
    pallas_call x1, Pallas kernels, up_and_choose(): pl.pallas_call(up_kernel, out_shape=(jax.ShapeDtypeStruct((2, rows, weigh...  2.49 us
    ppermute x1, waiting for transfers between devices, swap(): return lax.ppermute(x, axis, [(i, i ^ mask) for i in range(devices)])  1.4 us
    pallas_call x1, Pallas kernels, pick_rows(): pl.pallas_call(functools.partial(pick_kernel, group_size), out_shape=jax....  1.17 us
    pallas_call x1, Pallas kernels, combine(): pl.pallas_call(combine_kernel, out_shape=jax.ShapeDtypeStruct((picks.shap...  0.82 us
  transfers between devices with their start and end apart: 1, of which 1 were waited for; matrix products, arithmetic and copies ran while one was open for 0% of the time, Pallas kernels for 0%

profile of v5, /device:TPU:0, one launch (start us, length us, event | category | flops | bytes accessed | tf_op | source)
XLA Modules:
  0.0 36.4 jit_solution(14129043795401893212)
XLA Ops:
  0.6 0.0 slice-start
  0.7 0.0 slice-start.1
  0.7 0.0 slice-start.2
  0.7 0.0 slice-start.3
  0.7 0.0 slice-start.4
  0.8 1.2 %pick_rows.1 = bf16[8,2,3584]{2,1,0:T(2,128)(2,1)S(1)} custom-call(s32[1,4]{1,0:T(1,128)} %bitcast.12, s32[3,6]{1,0:T(4,128)} %bitcast.8, bf16[6,3584]{1,0:T(8,128)(2,1)} %act_hbm.1), custom_call_target="tpu_custom_call" | custom-call | flops 99999997952 | bytes 120000000 | tf_op jit(solution)/shard_map/pick_rows/pallas_call | solution.py:74
  1.9 0.0 copy-start.6
  1.9 0.0 copy-start.7
  2.0 0.0 copy-start.9
  2.0 14.5 %all_to_all.10.came_ref = bf16[8,2,3584]{2,1,0:T(2,128)(2,1)S(1)} all-to-all(bf16[8,2,3584]{2,1,0:T(2,128)(2,1)S(1)} %pick_rows.1), channel_id=1, replica_groups=mesh['groups'=2,'wide'=8,'narrow'=2] {'wide'}, dimensions={0} | all-to-all | bytes 229376 | tf_op jit(solution)/shard_map/all_to_all | solution.py:284
  16.5 0.0 copy-done
  16.6 0.0 slice-start.5
  16.6 0.0 slice-start.6
  16.6 0.0 slice-start.7
  16.6 2.7 %gate_and_attend.1 = (f32[16,2560]{1,0:T(8,128)S(1)}, bf16[16,3584]{1,0:T(8,128)(2,1)S(1)}, bf16[4,8192]{1,0:T(4,128)(2,1)}) custom-call(bf16[8,2,3584]{2,1,0:T(2,128)(2,1)S(1)} %all_to_all.10.came_ref, bf16[3584,2560]{1,0:T(8,128)(2,1)S(1)} %copy-done, s32[1,4]{1,0:T(1,128)S(1)} %bitcast.11, bf16[4,32,256]{2,1,0:T(8,128)(2,1)S(1)} %copy-done.3, ...), custom_call_target="tpu_custom_call" | custom-call | tf_op jit(solution)/shard_map/gate_and_attend/pallas_call | solution.py:155
  19.3 0.0 slice-done.2
  19.4 0.0 slice-start.8
  19.4 0.0 slice-start.9
  19.4 2.5 %up_and_choose.1 = (f32[2,16,2560]{2,1,0:T(8,128)S(1)}, bf16[2,16,2560]{2,1,0:T(8,128)(2,1)S(1)}, bf16[6,16]{1,0:T(8,128)(2,1)S(1)}, f32[6,1]{1,0:T(8,128)S(1)}) custom-call(bf16[16,3584]{1,0:T(8,128)(2,1)S(1)} %get-tuple-element.9.rows_ref, bf16[3584,2560]{1,0:T(8,128)(2,1)S(1)} %bitcast.5, f32[16,2560]{1,0:T(8,128)S(1)} %get-tuple-element.10.gate_ref, ...), custom_call_target="tpu_custom_call" | custom-call | tf_op jit(solution)/shard_map/up_and_choose/pallas_call | solution.py:206
  21.9 0.0 collective-permute-start
  21.9 1.4 %collective-permute-done.there_ref = bf16[2,16,2560]{2,1,0:T(8,128)(2,1)S(1)} collective-permute-done((bf16[2,16,2560]{2,1,0:T(8,128)(2,1)S(1)}, bf16[2,16,2560]{2,1,0:T(8,128)(2,1)S(1)}, u32[]{:S(2)}, u32[]{:S(2)}) %collective-permute-start) | collective-permute-done | bytes 163872 | tf_op jit(solution)/shard_map/ppermute | solution.py:260
  23.4 2.5 %down.1 = bf16[8,2,3584]{2,1,0:T(2,128)(2,1)S(1)} custom-call(f32[2,16,2560]{2,1,0:T(8,128)S(1)} %get-tuple-element.13.here_ref, bf16[2,16,2560]{2,1,0:T(8,128)(2,1)S(1)} %collective-permute-done.there_ref, bf16[2560,3584]{1,0:T(8,128)(2,1)S(1)} %bitcast.7), custom_call_target="tpu_custom_call" | custom-call | tf_op jit(solution)/shard_map/down/pallas_call | solution.py:232
  25.9 9.7 %all_to_all.11.back_ref = bf16[8,2,3584]{2,1,0:T(2,128)(2,1)S(1)} all-to-all(bf16[8,2,3584]{2,1,0:T(2,128)(2,1)S(1)} %down.1), channel_id=1, replica_groups=mesh['groups'=2,'wide'=8,'narrow'=2] {'wide'}, dimensions={0} | all-to-all | bytes 229376 | tf_op jit(solution)/shard_map/all_to_all | solution.py:292
  35.6 0.8 %combine.1 = bf16[6,3584]{1,0:T(8,128)(2,1)} custom-call(bf16[6,16]{1,0:T(8,128)(2,1)S(1)} %get-tuple-element.11.picks_ref, f32[6,1]{1,0:T(8,128)S(1)} %get-tuple-element.12.weight_ref, bf16[8,2,3584]{2,1,0:T(2,128)(2,1)S(1)} %all_to_all.11.back_ref), custom_call_target="tpu_custom_call" | custom-call | tf_op jit(solution)/shard_map/combine/pallas_call | solution.py:249
  (27 shorter events, 0.1 us)
Async XLA Ops:
  0.6 18.7 %slice-start = ((s8[18350080]{0:T(1024)(128)(4,1)}), s8[4194304]{0:T(1024)(128)(4,1)S(1)}, s32[]{:S(2)}) async-start(s8[18350080]{0:T(1024)(128)(4,1)} %bitcast.4), calls=%async_computation.2 | async-start | bytes 8388608
  0.6 15.9 %copy-start = (bf16[3584,2560]{1,0:T(8,128)(2,1)S(1)}, bf16[3584,2560]{1,0:T(8,128)(2,1)}, u32[]{:S(2)}) copy-start(bf16[3584,2560]{1,0:T(8,128)(2,1)} %weight_ref.2) | copy-start | bytes 55050244
  0.7 15.9 %copy-start.1 = (bf16[4,256,256]{2,1,0:T(8,128)(2,1)S(1)}, bf16[4,256,256]{2,1,0:T(8,128)(2,1)}, u32[]{:S(2)}) copy-start(bf16[4,256,256]{2,1,0:T(8,128)(2,1)} %refs_4_.1) | copy-start | bytes 1572868
  0.7 15.9 %copy-start.2 = (bf16[4,256,256]{2,1,0:T(8,128)(2,1)S(1)}, bf16[4,256,256]{2,1,0:T(8,128)(2,1)}, u32[]{:S(2)}) copy-start(bf16[4,256,256]{2,1,0:T(8,128)(2,1)} %refs_5_.1) | copy-start | bytes 1572868
  0.7 15.9 %copy-start.3 = (bf16[4,32,256]{2,1,0:T(8,128)(2,1)S(1)}, bf16[4,32,256]{2,1,0:T(8,128)(2,1)}, u32[]{:S(2)}) copy-start(bf16[4,32,256]{2,1,0:T(8,128)(2,1)} %refs_1_.1) | copy-start | bytes 196612
  0.7 15.9 %copy-start.4 = (bf16[4,256]{1,0:T(4,128)(2,1)S(1)}, bf16[4,256]{1,0:T(4,128)(2,1)}, u32[]{:S(2)}) copy-start(bf16[4,256]{1,0:T(4,128)(2,1)} %refs_2_.1) | copy-start | bytes 6148
  0.7 15.9 %copy-start.5 = (bf16[4,256]{1,0:T(4,128)(2,1)S(1)}, bf16[4,256]{1,0:T(4,128)(2,1)}, u32[]{:S(2)}) copy-start(bf16[4,256]{1,0:T(4,128)(2,1)} %refs_3_.1) | copy-start | bytes 6148
  0.7 15.9 %copy-start.8 = (s32[4]{0:T(128)S(1)}, s32[4]{0:T(128)}, u32[]{:S(2)}) copy-start(s32[4]{0:T(128)} %param.25) | copy-start | bytes 52
  0.7 18.6 %slice-start.1 = ((s8[18350080]{0:T(1024)(128)(4,1)}), s8[4194304]{0:T(1024)(128)(4,1)S(1)}, s32[]{:S(2)}) async-start(s8[18350080]{0:T(1024)(128)(4,1)} %bitcast.4), calls=%async_computation.3 | async-start | bytes 8388608
  0.7 18.6 %slice-start.2 = ((s8[18350080]{0:T(1024)(128)(4,1)}), s8[4194304]{0:T(1024)(128)(4,1)S(1)}, s32[]{:S(2)}) async-start(s8[18350080]{0:T(1024)(128)(4,1)} %bitcast.4), calls=%async_computation.4 | async-start | bytes 8388608
  0.7 18.6 %slice-start.3 = ((s8[18350080]{0:T(1024)(128)(4,1)}), s8[4194304]{0:T(1024)(128)(4,1)S(1)}, s32[]{:S(2)}) async-start(s8[18350080]{0:T(1024)(128)(4,1)} %bitcast.4), calls=%async_computation.5 | async-start | bytes 8388608
  0.7 18.6 %slice-start.4 = ((s8[18350080]{0:T(1024)(128)(4,1)}), s8[1572864]{0:T(1024)(128)(4,1)S(1)}, s32[]{:S(2)}) async-start(s8[18350080]{0:T(1024)(128)(4,1)} %bitcast.4), calls=%async_computation.6 | async-start | bytes 3145728
  1.9 17.4 %copy-start.6 = (s32[6,3]{0,1:T(4,128)S(1)}, s32[6,3]{0,1:T(4,128)}, u32[]{:S(2)}) copy-start(s32[6,3]{0,1:T(4,128)} %param.14) | copy-start | bytes 220
  1.9 17.4 %copy-start.7 = (f32[6,3]{0,1:T(4,128)S(1)}, f32[6,3]{0,1:T(4,128)}, u32[]{:S(2)}) copy-start(f32[6,3]{0,1:T(4,128)} %param.15) | copy-start | bytes 220
  2.0 17.4 %copy-start.9 = (s32[4]{0:T(128)S(1)}, s32[4]{0:T(128)}, u32[]{:S(2)}) copy-start(s32[4]{0:T(128)} %param.16) | copy-start | bytes 52
  16.6 6.8 %slice-start.5 = ((s8[18350080]{0:T(1024)(128)(4,1)}), s8[4194304]{0:T(1024)(128)(4,1)S(1)}, s32[]{:S(2)}) async-start(s8[18350080]{0:T(1024)(128)(4,1)} %bitcast.6), calls=%async_computation.7 | async-start | bytes 8388608
  16.6 6.7 %slice-start.6 = ((s8[18350080]{0:T(1024)(128)(4,1)}), s8[4194304]{0:T(1024)(128)(4,1)S(1)}, s32[]{:S(2)}) async-start(s8[18350080]{0:T(1024)(128)(4,1)} %bitcast.6), calls=%async_computation.8 | async-start | bytes 8388608
  16.6 6.7 %slice-start.7 = ((s8[18350080]{0:T(1024)(128)(4,1)}), s8[4194304]{0:T(1024)(128)(4,1)S(1)}, s32[]{:S(2)}) async-start(s8[18350080]{0:T(1024)(128)(4,1)} %bitcast.6), calls=%async_computation.9 | async-start | bytes 8388608
  19.4 3.9 %slice-start.8 = ((s8[18350080]{0:T(1024)(128)(4,1)}), s8[4194304]{0:T(1024)(128)(4,1)S(1)}, s32[]{:S(2)}) async-start(s8[18350080]{0:T(1024)(128)(4,1)} %bitcast.6), calls=%async_computation.10 | async-start | bytes 8388608
  19.4 3.9 %slice-start.9 = ((s8[18350080]{0:T(1024)(128)(4,1)}), s8[1572864]{0:T(1024)(128)(4,1)S(1)}, s32[]{:S(2)}) async-start(s8[18350080]{0:T(1024)(128)(4,1)} %bitcast.6), calls=%async_computation.11 | async-start | bytes 3145728
  21.9 1.4 %collective-permute-start = (bf16[2,16,2560]{2,1,0:T(8,128)(2,1)S(1)}, bf16[2,16,2560]{2,1,0:T(8,128)(2,1)S(1)}, u32[]{:S(2)}, u32[]{:S(2)}) collective-permute-start(bf16[2,16,2560]{2,1,0:T(8,128)(2,1)S(1)} %get-tuple-element.14), channel_id=1, source_target_pairs={{0,1},{1,0},{2,3},{3,2},{4,5},{5,4},{6,7},{7,6},{8,9},{9,8},{10,11... | collective-permute-start | bytes 491528 | tf_op jit(solution)/shard_map/ppermute | solution.py:260

commit v6 on v4

--- a/solution.py
+++ b/solution.py
@@ -90,7 +90,7 @@
     )(*in_hbm(owners, routes_t, act_rows))
 
 
-def attention_steps(lengths_ref, q_ref, nk_ref, nv_ref, keys_ref, values_ref, out_ref, turn_ref):
+def attention_steps(lengths_ref, q_ref, nk_ref, keys_ref, prob_ref, own_ref):
     requests, heads, size = q_ref.shape
     scaling = size ** (-0.5)
     span = range(requests)
@@ -116,16 +116,32 @@
     score = jnp.exp(score - top)
     own = jnp.exp(own - top)
     total = jnp.sum(score, axis=1, keepdims=True) + own
-    prob = (score / total).astype(BF16)
-    own = (own / total).astype(BF16).astype(F32)
-    yield
-    for r in span:
+    prob_ref[...] = (score / total).astype(BF16)
+    own_ref[...] = (own / total).astype(BF16).astype(F32)
+
+
+def mix_kernel(prob_ref, own_ref, nv_ref, values_ref, out_ref, turn_ref):
+    heads, requests, size = turn_ref.shape
+    for r in range(requests):
         part = slice(r * heads, (r + 1) * heads)
-        mixed = jnp.dot(prob[part], values_ref[r], preferred_element_type=F32)
-        turn_ref[:, r, :] = mixed + own[part] * nv_ref[r : r + 1, :].astype(F32)
-    yield
+        mixed = jnp.dot(prob_ref[part, :], values_ref[r], preferred_element_type=F32)
+        turn_ref[:, r, :] = mixed + own_ref[part, :] * nv_ref[r : r + 1, :].astype(F32)
     for h in range(heads):
         out_ref[:, h * size : (h + 1) * size] = turn_ref[h].astype(BF16)
+
+
+def mix(prob, own, new_values, value_cache):
+    requests, _, size = value_cache.shape
+    heads = prob.shape[0] // requests
+    return pl.pallas_call(
+        mix_kernel,
+        out_shape=jax.ShapeDtypeStruct((requests, heads * size), BF16),
+        in_specs=[VMEM] * 4,
+        out_specs=VMEM,
+        scratch_shapes=[pltpu.VMEM((heads, requests, size), F32)],
+        compiler_params=params(2),
+        name="mix",
+    )(prob, own, *in_vmem(new_values, value_cache))
 
 
 def stacked(rows_ref):
@@ -134,10 +150,10 @@
 
 
 def gate_kernel(came_ref, weight_ref, *refs):
-    out_ref, rows_ref, context_ref, turn_ref = refs[6:]
+    out_ref, rows_ref, prob_ref, own_ref = refs[4:]
     rows = stacked(came_ref)
     rows_ref[...] = rows
-    steps = attention_steps(*refs[:6], context_ref, turn_ref)
+    steps = attention_steps(*refs[:4], prob_ref, own_ref)
     hidden = weight_ref.shape[1]
     width = next(n for n in (256, 256, hidden) if hidden % n == 0)
     for n in range(0, hidden, width):
@@ -151,17 +167,17 @@
 
 def gate_and_attend(came, weight, lengths, *operands):
     rows = came.shape[0] * CAP
-    requests, heads, size = operands[0].shape
+    requests, heads, _ = operands[0].shape
     return pl.pallas_call(
         gate_kernel,
         out_shape=(
             jax.ShapeDtypeStruct((rows, weight.shape[1]), F32),
             jax.ShapeDtypeStruct((rows, weight.shape[0]), BF16),
-            jax.ShapeDtypeStruct((requests, heads * size), BF16),
+            jax.ShapeDtypeStruct((requests * heads, operands[2].shape[1]), BF16),
+            jax.ShapeDtypeStruct((requests * heads, 1), F32),
         ),
-        in_specs=[VMEM] * 8,
-        out_specs=(VMEM,) * 3,
-        scratch_shapes=[pltpu.VMEM((heads, requests, size), F32)],
+        in_specs=[VMEM] * 6,
+        out_specs=(VMEM,) * 4,
         compiler_params=params(4, rows),
         name="gate_and_attend",
     )(came, weight, lengths, *in_vmem(*operands))
@@ -276,11 +292,15 @@
     owners, lengths = owners[None], lengths[None]
     picked = pick_rows(owners, routes_t, act_rows, group_size)
     came = lax.all_to_all(picked, "wide", split_axis=0, concat_axis=0, tiled=True)
-    gate, came_rows, context = gate_and_attend(
-        came, w_gate, lengths, queries, new_keys, new_values, key_cache, value_cache
+    gate, came_rows, prob, own = gate_and_attend(
+        came, w_gate, lengths, queries, new_keys, key_cache
     )
     sums, picks, weight = up_and_choose(came_rows, w_up, gate, owners, routes_t, weights_t)
-    partial_value = down(sums, swap(sums, "narrow", 2, 1), w_down)
+    sums, prob, own = lax.optimization_barrier((sums, prob, own))
+    context = mix(prob, own, new_values, value_cache)
+    there = swap(sums, "narrow", 2, 1)
+    there, context = lax.optimization_barrier((there, context))
+    partial_value = down(sums, there, w_down)
     back = lax.all_to_all(partial_value, "wide", split_axis=0, concat_axis=0, tiled=True)
     return (combine(picks, weight, back), context)
 

time: 36.8 us -> 36.7 us (level)
  waiting for transfers between devices: 1.63 us -> 0.75 us
  Pallas kernels: 9.69 us -> 10.5 us
    ppermute x1, waiting for transfers between devices: 1.63 us -> 0.75 us  [swap(): return lax.ppermute(x, axis, [(i, i ^ mask) for i in range(devices)])]
    pallas_call x0 -> x1, Pallas kernels: none -> 0.87 us  [mix(): pl.pallas_call(mix_kernel, out_shape=jax.ShapeDtypeStruct((requests, head...]
  transfers between devices with their start and end apart: 1 -> 1, of which waited for: 1 -> 1; matrix products, arithmetic and copies ran while one was open for 0% -> 0% of each run, Pallas kernels for 0% -> 2%
where the time goes in v6:
time: 36.7 us; the launch traced here: 36.5 us
  blocking collectives  24.2 us (66%)
  Pallas kernels  10.5 us (29%)
  between operations  0.91 us (2%)
  waiting for transfers between devices  0.75 us (2%)
    all_to_all x1, blocking collectives, per_device(): lax.all_to_all(picked, 'wide', split_axis=0, concat_axis=0, tiled=True)  14.5 us
    all_to_all x1, blocking collectives, per_device(): lax.all_to_all(partial_value, 'wide', split_axis=0, concat_axis=0, tiled=...  9.7 us
    pallas_call x1, Pallas kernels, gate_and_attend(): pl.pallas_call(gate_kernel, out_shape=(jax.ShapeDtypeStruct((rows, weight...  2.64 us
    pallas_call x1, Pallas kernels, down(): pl.pallas_call(down_kernel, out_shape=jax.ShapeDtypeStruct((rows // CAP,...  2.5 us
    pallas_call x1, Pallas kernels, up_and_choose(): pl.pallas_call(up_kernel, out_shape=(jax.ShapeDtypeStruct((2, rows, weigh...  2.48 us
    pallas_call x1, Pallas kernels, pick_rows(): pl.pallas_call(functools.partial(pick_kernel, group_size), out_shape=jax....  1.17 us
    pallas_call x1, Pallas kernels, mix(): pl.pallas_call(mix_kernel, out_shape=jax.ShapeDtypeStruct((requests, head...  0.87 us
    pallas_call x1, Pallas kernels, combine(): pl.pallas_call(combine_kernel, out_shape=jax.ShapeDtypeStruct((picks.shap...  0.82 us
  transfers between devices with their start and end apart: 1, of which 1 were waited for; matrix products, arithmetic and copies ran while one was open for 0% of the time, Pallas kernels for 2%

profile of v6, /device:TPU:0, one launch (start us, length us, event | category | flops | bytes accessed | tf_op | source)
XLA Modules:
  0.0 36.5 jit_solution(14747101028847100782)
XLA Ops:
  0.6 0.0 slice-start
  0.7 0.0 slice-start.1
  0.7 0.0 slice-start.2
  0.7 0.0 slice-start.3
  0.7 1.2 %pick_rows.1 = bf16[8,2,3584]{2,1,0:T(2,128)(2,1)S(1)} custom-call(s32[1,4]{1,0:T(1,128)} %bitcast.12, s32[3,6]{1,0:T(4,128)} %bitcast.8, bf16[6,3584]{1,0:T(8,128)(2,1)} %act_hbm.1), custom_call_target="tpu_custom_call" | custom-call | flops 99999997952 | bytes 120000000 | tf_op jit(solution)/shard_map/pick_rows/pallas_call | solution.py:74
  1.9 0.0 copy-start.6
  1.9 0.0 copy-start.7
  1.9 0.0 copy-start.9
  2.0 14.5 %all_to_all.10.came_ref = bf16[8,2,3584]{2,1,0:T(2,128)(2,1)S(1)} all-to-all(bf16[8,2,3584]{2,1,0:T(2,128)(2,1)S(1)} %pick_rows.1), channel_id=1, replica_groups=mesh['groups'=2,'wide'=8,'narrow'=2] {'wide'}, dimensions={0} | all-to-all | bytes 229376 | tf_op jit(solution)/shard_map/all_to_all | solution.py:294
  16.5 0.0 copy-start.2
  16.5 0.0 copy-start.5
  16.6 0.0 slice-start.5
  16.6 0.0 slice-start.6
  16.6 0.0 slice-start.7
  16.6 2.6 %gate_and_attend.1 = (f32[16,2560]{1,0:T(8,128)S(1)}, bf16[16,3584]{1,0:T(8,128)(2,1)S(1)}, bf16[128,256]{1,0:T(8,128)(2,1)S(1)}, f32[128,1]{1,0:T(8,128)S(1)}) custom-call(bf16[8,2,3584]{2,1,0:T(2,128)(2,1)S(1)} %all_to_all.10.came_ref, bf16[3584,2560]{1,0:T(8,128)(2,1)S(1)} %copy-done, s32[1,4]{1,0:T(1,128)S(1)} %bitcast.11, ...), custom_call_target="tpu_custom_call" | custom-call | tf_op jit(solution)/shard_map/gate_and_attend/pallas_call | solution.py:171
  19.2 0.0 slice-done.2
  19.3 0.0 slice-start.8
  19.3 2.5 %up_and_choose.1 = (f32[2,16,2560]{2,1,0:T(8,128)S(1)}, bf16[6,16]{1,0:T(8,128)(2,1)S(1)}, f32[6,1]{1,0:T(8,128)S(1)}) custom-call(bf16[16,3584]{1,0:T(8,128)(2,1)S(1)} %get-tuple-element.14.rows_ref, bf16[3584,2560]{1,0:T(8,128)(2,1)S(1)} %bitcast.5, f32[16,2560]{1,0:T(8,128)S(1)} %get-tuple-element.15.gate_ref, s32[1,4]{1,0:T(1,128)S(1)} %bitcast.13, ...), custom_call_target="tpu_custom_call" | custom-call | tf_op jit(solution)/shard_map/up_and_choose/pallas_call | solution.py:217
  21.8 0.0 copy-done.5
  21.8 0.9 %mix.1 = bf16[4,8192]{1,0:T(4,128)(2,1)} custom-call(bf16[128,256]{1,0:T(8,128)(2,1)S(1)} %get-tuple-element.22.prob_ref, f32[128,1]{1,0:T(8,128)S(1)} %get-tuple-element.23.own_ref, bf16[4,256]{1,0:T(4,128)(2,1)S(1)} %copy-done.5, bf16[4,256,256]{2,1,0:T(8,128)(2,1)S(1)} %copy-done.2), custom_call_target="tpu_custom_call" | custom-call | tf_op jit(solution)/shard_map/mix/pallas_call | solution.py:136
  22.7 0.7 %collective-permute-done.there_ref = f32[2,16,2560]{2,1,0:T(8,128)S(1)} collective-permute-done((f32[2,16,2560]{2,1,0:T(8,128)S(1)}, f32[2,16,2560]{2,1,0:T(8,128)S(1)}, u32[]{:S(2)}, u32[]{:S(2)}) %collective-permute-start) | collective-permute-done | bytes 327712 | tf_op jit(solution)/shard_map/ppermute | solution.py:270
  23.5 2.5 %down.1 = bf16[8,2,3584]{2,1,0:T(2,128)(2,1)S(1)} custom-call(f32[2,16,2560]{2,1,0:T(8,128)S(1)} %get-tuple-element.21.here_ref, f32[2,16,2560]{2,1,0:T(8,128)S(1)} %collective-permute-done.there_ref, bf16[2560,3584]{1,0:T(8,128)(2,1)S(1)} %bitcast.7), custom_call_target="tpu_custom_call" | custom-call | tf_op jit(solution)/shard_map/down/pallas_call | solution.py:242
  26.0 9.7 %all_to_all.11.back_ref = bf16[8,2,3584]{2,1,0:T(2,128)(2,1)S(1)} all-to-all(bf16[8,2,3584]{2,1,0:T(2,128)(2,1)S(1)} %down.1), channel_id=1, replica_groups=mesh['groups'=2,'wide'=8,'narrow'=2] {'wide'}, dimensions={0} | all-to-all | bytes 229376 | tf_op jit(solution)/shard_map/all_to_all | solution.py:304
  35.7 0.8 %combine.1 = bf16[6,3584]{1,0:T(8,128)(2,1)} custom-call(bf16[6,16]{1,0:T(8,128)(2,1)S(1)} %get-tuple-element.16.picks_ref, f32[6,1]{1,0:T(8,128)S(1)} %get-tuple-element.17.weight_ref, bf16[8,2,3584]{2,1,0:T(2,128)(2,1)S(1)} %all_to_all.11.back_ref), custom_call_target="tpu_custom_call" | custom-call | tf_op jit(solution)/shard_map/combine/pallas_call | solution.py:259
  (28 shorter events, 0.1 us)
Async XLA Ops:
  0.6 18.6 %slice-start = ((s8[18350080]{0:T(1024)(128)(4,1)}), s8[4194304]{0:T(1024)(128)(4,1)S(1)}, s32[]{:S(2)}) async-start(s8[18350080]{0:T(1024)(128)(4,1)} %bitcast.4), calls=%async_computation.2 | async-start | bytes 8388608
  0.6 15.9 %copy-start = (bf16[3584,2560]{1,0:T(8,128)(2,1)S(1)}, bf16[3584,2560]{1,0:T(8,128)(2,1)}, u32[]{:S(2)}) copy-start(bf16[3584,2560]{1,0:T(8,128)(2,1)} %weight_ref.2) | copy-start | bytes 55050244
  0.7 15.9 %copy-start.1 = (bf16[4,256,256]{2,1,0:T(8,128)(2,1)S(1)}, bf16[4,256,256]{2,1,0:T(8,128)(2,1)}, u32[]{:S(2)}) copy-start(bf16[4,256,256]{2,1,0:T(8,128)(2,1)} %refs_3_.1) | copy-start | bytes 1572868
  0.7 15.8 %copy-start.3 = (bf16[4,32,256]{2,1,0:T(8,128)(2,1)S(1)}, bf16[4,32,256]{2,1,0:T(8,128)(2,1)}, u32[]{:S(2)}) copy-start(bf16[4,32,256]{2,1,0:T(8,128)(2,1)} %refs_1_.1) | copy-start | bytes 196612
  0.7 15.8 %copy-start.4 = (bf16[4,256]{1,0:T(4,128)(2,1)S(1)}, bf16[4,256]{1,0:T(4,128)(2,1)}, u32[]{:S(2)}) copy-start(bf16[4,256]{1,0:T(4,128)(2,1)} %refs_2_.1) | copy-start | bytes 6148
  0.7 15.8 %copy-start.8 = (s32[4]{0:T(128)S(1)}, s32[4]{0:T(128)}, u32[]{:S(2)}) copy-start(s32[4]{0:T(128)} %param.25) | copy-start | bytes 52
  0.7 18.5 %slice-start.1 = ((s8[18350080]{0:T(1024)(128)(4,1)}), s8[4194304]{0:T(1024)(128)(4,1)S(1)}, s32[]{:S(2)}) async-start(s8[18350080]{0:T(1024)(128)(4,1)} %bitcast.4), calls=%async_computation.3 | async-start | bytes 8388608
  0.7 18.5 %slice-start.2 = ((s8[18350080]{0:T(1024)(128)(4,1)}), s8[4194304]{0:T(1024)(128)(4,1)S(1)}, s32[]{:S(2)}) async-start(s8[18350080]{0:T(1024)(128)(4,1)} %bitcast.4), calls=%async_computation.4 | async-start | bytes 8388608
  0.7 18.5 %slice-start.3 = ((s8[18350080]{0:T(1024)(128)(4,1)}), s8[4194304]{0:T(1024)(128)(4,1)S(1)}, s32[]{:S(2)}) async-start(s8[18350080]{0:T(1024)(128)(4,1)} %bitcast.4), calls=%async_computation.5 | async-start | bytes 8388608
  0.7 18.5 %slice-start.4 = ((s8[18350080]{0:T(1024)(128)(4,1)}), s8[1572864]{0:T(1024)(128)(4,1)S(1)}, s32[]{:S(2)}) async-start(s8[18350080]{0:T(1024)(128)(4,1)} %bitcast.4), calls=%async_computation.6 | async-start | bytes 3145728
  1.9 17.4 %copy-start.6 = (s32[6,3]{0,1:T(4,128)S(1)}, s32[6,3]{0,1:T(4,128)}, u32[]{:S(2)}) copy-start(s32[6,3]{0,1:T(4,128)} %param.14) | copy-start | bytes 220
  1.9 17.3 %copy-start.7 = (f32[6,3]{0,1:T(4,128)S(1)}, f32[6,3]{0,1:T(4,128)}, u32[]{:S(2)}) copy-start(f32[6,3]{0,1:T(4,128)} %param.15) | copy-start | bytes 220
  1.9 17.3 %copy-start.9 = (s32[4]{0:T(128)S(1)}, s32[4]{0:T(128)}, u32[]{:S(2)}) copy-start(s32[4]{0:T(128)} %param.16) | copy-start | bytes 52
  16.5 5.3 %copy-start.2 = (bf16[4,256,256]{2,1,0:T(8,128)(2,1)S(1)}, bf16[4,256,256]{2,1,0:T(8,128)(2,1)}, u32[]{:S(2)}) copy-start(bf16[4,256,256]{2,1,0:T(8,128)(2,1)} %values_ref.1) | copy-start | bytes 1572868
  16.5 5.3 %copy-start.5 = (bf16[4,256]{1,0:T(4,128)(2,1)S(1)}, bf16[4,256]{1,0:T(4,128)(2,1)}, u32[]{:S(2)}) copy-start(bf16[4,256]{1,0:T(4,128)(2,1)} %nv_ref.1) | copy-start | bytes 6148
  16.6 6.9 %slice-start.5 = ((s8[18350080]{0:T(1024)(128)(4,1)}), s8[4194304]{0:T(1024)(128)(4,1)S(1)}, s32[]{:S(2)}) async-start(s8[18350080]{0:T(1024)(128)(4,1)} %bitcast.6), calls=%async_computation.7 | async-start | bytes 8388608
  16.6 6.9 %slice-start.6 = ((s8[18350080]{0:T(1024)(128)(4,1)}), s8[4194304]{0:T(1024)(128)(4,1)S(1)}, s32[]{:S(2)}) async-start(s8[18350080]{0:T(1024)(128)(4,1)} %bitcast.6), calls=%async_computation.8 | async-start | bytes 8388608
  16.6 6.9 %slice-start.7 = ((s8[18350080]{0:T(1024)(128)(4,1)}), s8[4194304]{0:T(1024)(128)(4,1)S(1)}, s32[]{:S(2)}) async-start(s8[18350080]{0:T(1024)(128)(4,1)} %bitcast.6), calls=%async_computation.9 | async-start | bytes 8388608
  19.3 4.2 %slice-start.8 = ((s8[18350080]{0:T(1024)(128)(4,1)}), s8[4194304]{0:T(1024)(128)(4,1)S(1)}, s32[]{:S(2)}) async-start(s8[18350080]{0:T(1024)(128)(4,1)} %bitcast.6), calls=%async_computation.10 | async-start | bytes 8388608
  19.3 4.1 %slice-start.9 = ((s8[18350080]{0:T(1024)(128)(4,1)}), s8[1572864]{0:T(1024)(128)(4,1)S(1)}, s32[]{:S(2)}) async-start(s8[18350080]{0:T(1024)(128)(4,1)} %bitcast.6), calls=%async_computation.11 | async-start | bytes 3145728
  21.8 1.6 %collective-permute-start = (f32[2,16,2560]{2,1,0:T(8,128)S(1)}, f32[2,16,2560]{2,1,0:T(8,128)S(1)}, u32[]{:S(2)}, u32[]{:S(2)}) collective-permute-start(f32[2,16,2560]{2,1,0:T(8,128)S(1)} %get-tuple-element.21.here_ref), channel_id=1, source_target_pairs={{0,1},{1,0},{2,3},{3,2},{4,5},{5,4},{6,7},{7,6},{8,9},{9,8},{10,11... | collective-permute-start | bytes 983048 | tf_op jit(solution)/shard_map/ppermute | solution.py:270

commit v7 on v6

--- a/solution.py
+++ b/solution.py
@@ -113,19 +113,20 @@
     own = jnp.concatenate(owns, axis=0) * scaling
     top = jnp.maximum(jnp.max(score, axis=1, keepdims=True), own)
     yield
-    score = jnp.exp(score - top)
-    own = jnp.exp(own - top)
-    total = jnp.sum(score, axis=1, keepdims=True) + own
-    prob_ref[...] = (score / total).astype(BF16)
-    own_ref[...] = (own / total).astype(BF16).astype(F32)
+    prob_ref[...] = jnp.exp(score - top)
+    own_ref[...] = jnp.exp(own - top)
 
 
 def mix_kernel(prob_ref, own_ref, nv_ref, values_ref, out_ref, turn_ref):
     heads, requests, size = turn_ref.shape
+    score, own = prob_ref[...], own_ref[...]
+    total = jnp.sum(score, axis=1, keepdims=True) + own
+    prob = (score / total).astype(BF16)
+    own = (own / total).astype(BF16).astype(F32)
     for r in range(requests):
         part = slice(r * heads, (r + 1) * heads)
-        mixed = jnp.dot(prob_ref[part, :], values_ref[r], preferred_element_type=F32)
-        turn_ref[:, r, :] = mixed + own_ref[part, :] * nv_ref[r : r + 1, :].astype(F32)
+        mixed = jnp.dot(prob[part], values_ref[r], preferred_element_type=F32)
+        turn_ref[:, r, :] = mixed + own[part] * nv_ref[r : r + 1, :].astype(F32)
     for h in range(heads):
         out_ref[:, h * size : (h + 1) * size] = turn_ref[h].astype(BF16)
 
@@ -173,7 +174,7 @@
         out_shape=(
             jax.ShapeDtypeStruct((rows, weight.shape[1]), F32),
             jax.ShapeDtypeStruct((rows, weight.shape[0]), BF16),
-            jax.ShapeDtypeStruct((requests * heads, operands[2].shape[1]), BF16),
+            jax.ShapeDtypeStruct((requests * heads, operands[2].shape[1]), F32),
             jax.ShapeDtypeStruct((requests * heads, 1), F32),
         ),
         in_specs=[VMEM] * 6,

time: 36.7 us -> 36.7 us (level)
  transfers between devices with their start and end apart: 1 -> 1, of which waited for: 1 -> 1; matrix products, arithmetic and copies ran while one was open for 0% -> 0% of each run, Pallas kernels for 2% -> 3%
where the time goes in v7:
time: 36.7 us; the launch traced here: 36.5 us
  blocking collectives  24.2 us (66%)
  Pallas kernels  10.6 us (29%)
  between operations  0.91 us (2%)
  waiting for transfers between devices  0.61 us (2%)
    all_to_all x1, blocking collectives, per_device(): lax.all_to_all(picked, 'wide', split_axis=0, concat_axis=0, tiled=True)  14.5 us
    all_to_all x1, blocking collectives, per_device(): lax.all_to_all(partial_value, 'wide', split_axis=0, concat_axis=0, tiled=...  9.7 us
    pallas_call x1, Pallas kernels, gate_and_attend(): pl.pallas_call(gate_kernel, out_shape=(jax.ShapeDtypeStruct((rows, weight...  2.64 us
    pallas_call x1, Pallas kernels, down(): pl.pallas_call(down_kernel, out_shape=jax.ShapeDtypeStruct((rows // CAP,...  2.5 us
    pallas_call x1, Pallas kernels, up_and_choose(): pl.pallas_call(up_kernel, out_shape=(jax.ShapeDtypeStruct((2, rows, weigh...  2.48 us
    pallas_call x1, Pallas kernels, pick_rows(): pl.pallas_call(functools.partial(pick_kernel, group_size), out_shape=jax....  1.17 us
    pallas_call x1, Pallas kernels, mix(): pl.pallas_call(mix_kernel, out_shape=jax.ShapeDtypeStruct((requests, head...  1.01 us
    pallas_call x1, Pallas kernels, combine(): pl.pallas_call(combine_kernel, out_shape=jax.ShapeDtypeStruct((picks.shap...  0.82 us
  transfers between devices with their start and end apart: 1, of which 1 were waited for; matrix products, arithmetic and copies ran while one was open for 0% of the time, Pallas kernels for 3%

profile of v7, /device:TPU:0, one launch (start us, length us, event | category | flops | bytes accessed | tf_op | source)
XLA Modules:
  0.0 36.5 jit_solution(4393744266821642492)
XLA Ops:
  0.6 0.0 slice-start
  0.7 0.0 slice-start.1
  0.7 0.0 slice-start.2
  0.7 1.2 %pick_rows.1 = bf16[8,2,3584]{2,1,0:T(2,128)(2,1)S(1)} custom-call(s32[1,4]{1,0:T(1,128)} %bitcast.12, s32[3,6]{1,0:T(4,128)} %bitcast.8, bf16[6,3584]{1,0:T(8,128)(2,1)} %act_hbm.1), custom_call_target="tpu_custom_call" | custom-call | flops 99999997952 | bytes 120000000 | tf_op jit(solution)/shard_map/pick_rows/pallas_call | solution.py:74
  1.9 0.0 copy-start.6
  1.9 0.0 copy-start.7
  1.9 0.0 copy-start.9
  2.0 14.5 %all_to_all.10.came_ref = bf16[8,2,3584]{2,1,0:T(2,128)(2,1)S(1)} all-to-all(bf16[8,2,3584]{2,1,0:T(2,128)(2,1)S(1)} %pick_rows.1), channel_id=1, replica_groups=mesh['groups'=2,'wide'=8,'narrow'=2] {'wide'}, dimensions={0} | all-to-all | bytes 229376 | tf_op jit(solution)/shard_map/all_to_all | solution.py:295
  16.5 0.0 copy-start.2
  16.5 0.0 copy-start.5
  16.6 0.0 slice-start.5
  16.6 0.0 slice-start.6
  16.6 0.0 slice-start.7
  16.6 2.6 %gate_and_attend.1 = (f32[16,2560]{1,0:T(8,128)S(1)}, bf16[16,3584]{1,0:T(8,128)(2,1)S(1)}, f32[128,256]{1,0:T(8,128)S(1)}, f32[128,1]{1,0:T(8,128)S(1)}) custom-call(bf16[8,2,3584]{2,1,0:T(2,128)(2,1)S(1)} %all_to_all.10.came_ref, bf16[3584,2560]{1,0:T(8,128)(2,1)S(1)} %copy-done, s32[1,4]{1,0:T(1,128)S(1)} %bitcast.11, bf16[4,32,256]{2,1,0:T(8,128)(2,1)S(1)} %copy-done.3, ...), custom_call_target="tpu_custom_call" | custom-call | tf_op jit(solution)/shard_map/gate_and_attend/pallas_call | solution.py:172
  19.2 0.0 slice-done.2
  19.3 0.0 slice-start.8
  19.3 0.0 slice-start.9
  19.3 2.5 %up_and_choose.1 = (f32[2,16,2560]{2,1,0:T(8,128)S(1)}, bf16[6,16]{1,0:T(8,128)(2,1)S(1)}, f32[6,1]{1,0:T(8,128)S(1)}) custom-call(bf16[16,3584]{1,0:T(8,128)(2,1)S(1)} %get-tuple-element.14.rows_ref, bf16[3584,2560]{1,0:T(8,128)(2,1)S(1)} %bitcast.5, f32[16,2560]{1,0:T(8,128)S(1)} %get-tuple-element.15.gate_ref, s32[1,4]{1,0:T(1,128)S(1)} %bitcast.13, ...), custom_call_target="tpu_custom_call" | custom-call | tf_op jit(solution)/shard_map/up_and_choose/pallas_call | solution.py:218
  21.8 0.0 copy-done.5
  21.8 1.0 %mix.1 = bf16[4,8192]{1,0:T(4,128)(2,1)} custom-call(f32[128,256]{1,0:T(8,128)S(1)} %get-tuple-element.22.prob_ref, f32[128,1]{1,0:T(8,128)S(1)} %get-tuple-element.23.own_ref, bf16[4,256]{1,0:T(4,128)(2,1)S(1)} %copy-done.5, bf16[4,256,256]{2,1,0:T(8,128)(2,1)S(1)} %copy-done.2), custom_call_target="tpu_custom_call" | custom-call | tf_op jit(solution)/shard_map/mix/pallas_call | solution.py:137
  22.8 0.6 %collective-permute-done.there_ref = f32[2,16,2560]{2,1,0:T(8,128)S(1)} collective-permute-done((f32[2,16,2560]{2,1,0:T(8,128)S(1)}, f32[2,16,2560]{2,1,0:T(8,128)S(1)}, u32[]{:S(2)}, u32[]{:S(2)}) %collective-permute-start) | collective-permute-done | bytes 327712 | tf_op jit(solution)/shard_map/ppermute | solution.py:271
  23.5 2.5 %down.1 = bf16[8,2,3584]{2,1,0:T(2,128)(2,1)S(1)} custom-call(f32[2,16,2560]{2,1,0:T(8,128)S(1)} %get-tuple-element.21.here_ref, f32[2,16,2560]{2,1,0:T(8,128)S(1)} %collective-permute-done.there_ref, bf16[2560,3584]{1,0:T(8,128)(2,1)S(1)} %bitcast.7), custom_call_target="tpu_custom_call" | custom-call | tf_op jit(solution)/shard_map/down/pallas_call | solution.py:243
  26.0 9.7 %all_to_all.11.back_ref = bf16[8,2,3584]{2,1,0:T(2,128)(2,1)S(1)} all-to-all(bf16[8,2,3584]{2,1,0:T(2,128)(2,1)S(1)} %down.1), channel_id=1, replica_groups=mesh['groups'=2,'wide'=8,'narrow'=2] {'wide'}, dimensions={0} | all-to-all | bytes 229376 | tf_op jit(solution)/shard_map/all_to_all | solution.py:305
  35.7 0.8 %combine.1 = bf16[6,3584]{1,0:T(8,128)(2,1)} custom-call(bf16[6,16]{1,0:T(8,128)(2,1)S(1)} %get-tuple-element.16.picks_ref, f32[6,1]{1,0:T(8,128)S(1)} %get-tuple-element.17.weight_ref, bf16[8,2,3584]{2,1,0:T(2,128)(2,1)S(1)} %all_to_all.11.back_ref), custom_call_target="tpu_custom_call" | custom-call | tf_op jit(solution)/shard_map/combine/pallas_call | solution.py:260
  (28 shorter events, 0.1 us)
Async XLA Ops:
  0.6 18.6 %slice-start = ((s8[18350080]{0:T(1024)(128)(4,1)}), s8[4194304]{0:T(1024)(128)(4,1)S(1)}, s32[]{:S(2)}) async-start(s8[18350080]{0:T(1024)(128)(4,1)} %bitcast.4), calls=%async_computation.2 | async-start | bytes 8388608
  0.6 15.9 %copy-start = (bf16[3584,2560]{1,0:T(8,128)(2,1)S(1)}, bf16[3584,2560]{1,0:T(8,128)(2,1)}, u32[]{:S(2)}) copy-start(bf16[3584,2560]{1,0:T(8,128)(2,1)} %weight_ref.2) | copy-start | bytes 55050244
  0.7 15.9 %copy-start.1 = (bf16[4,256,256]{2,1,0:T(8,128)(2,1)S(1)}, bf16[4,256,256]{2,1,0:T(8,128)(2,1)}, u32[]{:S(2)}) copy-start(bf16[4,256,256]{2,1,0:T(8,128)(2,1)} %refs_3_.1) | copy-start | bytes 1572868
  0.7 15.8 %copy-start.3 = (bf16[4,32,256]{2,1,0:T(8,128)(2,1)S(1)}, bf16[4,32,256]{2,1,0:T(8,128)(2,1)}, u32[]{:S(2)}) copy-start(bf16[4,32,256]{2,1,0:T(8,128)(2,1)} %refs_1_.1) | copy-start | bytes 196612
  0.7 15.8 %copy-start.4 = (bf16[4,256]{1,0:T(4,128)(2,1)S(1)}, bf16[4,256]{1,0:T(4,128)(2,1)}, u32[]{:S(2)}) copy-start(bf16[4,256]{1,0:T(4,128)(2,1)} %refs_2_.1) | copy-start | bytes 6148
  0.7 15.8 %copy-start.8 = (s32[4]{0:T(128)S(1)}, s32[4]{0:T(128)}, u32[]{:S(2)}) copy-start(s32[4]{0:T(128)} %param.25) | copy-start | bytes 52
  0.7 18.5 %slice-start.1 = ((s8[18350080]{0:T(1024)(128)(4,1)}), s8[4194304]{0:T(1024)(128)(4,1)S(1)}, s32[]{:S(2)}) async-start(s8[18350080]{0:T(1024)(128)(4,1)} %bitcast.4), calls=%async_computation.3 | async-start | bytes 8388608
  0.7 18.5 %slice-start.2 = ((s8[18350080]{0:T(1024)(128)(4,1)}), s8[4194304]{0:T(1024)(128)(4,1)S(1)}, s32[]{:S(2)}) async-start(s8[18350080]{0:T(1024)(128)(4,1)} %bitcast.4), calls=%async_computation.4 | async-start | bytes 8388608
  0.7 18.5 %slice-start.3 = ((s8[18350080]{0:T(1024)(128)(4,1)}), s8[4194304]{0:T(1024)(128)(4,1)S(1)}, s32[]{:S(2)}) async-start(s8[18350080]{0:T(1024)(128)(4,1)} %bitcast.4), calls=%async_computation.5 | async-start | bytes 8388608
  0.7 18.5 %slice-start.4 = ((s8[18350080]{0:T(1024)(128)(4,1)}), s8[1572864]{0:T(1024)(128)(4,1)S(1)}, s32[]{:S(2)}) async-start(s8[18350080]{0:T(1024)(128)(4,1)} %bitcast.4), calls=%async_computation.6 | async-start | bytes 3145728
  1.9 17.3 %copy-start.6 = (s32[6,3]{0,1:T(4,128)S(1)}, s32[6,3]{0,1:T(4,128)}, u32[]{:S(2)}) copy-start(s32[6,3]{0,1:T(4,128)} %param.14) | copy-start | bytes 220
  1.9 17.3 %copy-start.7 = (f32[6,3]{0,1:T(4,128)S(1)}, f32[6,3]{0,1:T(4,128)}, u32[]{:S(2)}) copy-start(f32[6,3]{0,1:T(4,128)} %param.15) | copy-start | bytes 220
  1.9 17.3 %copy-start.9 = (s32[4]{0:T(128)S(1)}, s32[4]{0:T(128)}, u32[]{:S(2)}) copy-start(s32[4]{0:T(128)} %param.16) | copy-start | bytes 52
  16.5 5.3 %copy-start.2 = (bf16[4,256,256]{2,1,0:T(8,128)(2,1)S(1)}, bf16[4,256,256]{2,1,0:T(8,128)(2,1)}, u32[]{:S(2)}) copy-start(bf16[4,256,256]{2,1,0:T(8,128)(2,1)} %values_ref.1) | copy-start | bytes 1572868
  16.5 5.3 %copy-start.5 = (bf16[4,256]{1,0:T(4,128)(2,1)S(1)}, bf16[4,256]{1,0:T(4,128)(2,1)}, u32[]{:S(2)}) copy-start(bf16[4,256]{1,0:T(4,128)(2,1)} %nv_ref.1) | copy-start | bytes 6148
  16.6 6.9 %slice-start.5 = ((s8[18350080]{0:T(1024)(128)(4,1)}), s8[4194304]{0:T(1024)(128)(4,1)S(1)}, s32[]{:S(2)}) async-start(s8[18350080]{0:T(1024)(128)(4,1)} %bitcast.6), calls=%async_computation.7 | async-start | bytes 8388608
  16.6 6.9 %slice-start.6 = ((s8[18350080]{0:T(1024)(128)(4,1)}), s8[4194304]{0:T(1024)(128)(4,1)S(1)}, s32[]{:S(2)}) async-start(s8[18350080]{0:T(1024)(128)(4,1)} %bitcast.6), calls=%async_computation.8 | async-start | bytes 8388608
  16.6 6.9 %slice-start.7 = ((s8[18350080]{0:T(1024)(128)(4,1)}), s8[4194304]{0:T(1024)(128)(4,1)S(1)}, s32[]{:S(2)}) async-start(s8[18350080]{0:T(1024)(128)(4,1)} %bitcast.6), calls=%async_computation.9 | async-start | bytes 8388608
  19.3 4.2 %slice-start.8 = ((s8[18350080]{0:T(1024)(128)(4,1)}), s8[4194304]{0:T(1024)(128)(4,1)S(1)}, s32[]{:S(2)}) async-start(s8[18350080]{0:T(1024)(128)(4,1)} %bitcast.6), calls=%async_computation.10 | async-start | bytes 8388608
  19.3 4.1 %slice-start.9 = ((s8[18350080]{0:T(1024)(128)(4,1)}), s8[1572864]{0:T(1024)(128)(4,1)S(1)}, s32[]{:S(2)}) async-start(s8[18350080]{0:T(1024)(128)(4,1)} %bitcast.6), calls=%async_computation.11 | async-start | bytes 3145728
  21.8 1.6 %collective-permute-start = (f32[2,16,2560]{2,1,0:T(8,128)S(1)}, f32[2,16,2560]{2,1,0:T(8,128)S(1)}, u32[]{:S(2)}, u32[]{:S(2)}) collective-permute-start(f32[2,16,2560]{2,1,0:T(8,128)S(1)} %get-tuple-element.21.here_ref), channel_id=1, source_target_pairs={{0,1},{1,0},{2,3},{3,2},{4,5},{5,4},{6,7},{7,6},{8,9},{9,8},{10,11... | collective-permute-start | bytes 983048 | tf_op jit(solution)/shard_map/ppermute | solution.py:271
